TPU v7x, 32 devices: a whole 2x2x4 slice. The times are simulated.
32 devices in a mesh: groups: 2 (over x), ctx: 2 (over core), tp: 8 (over z, y).
Axes of the slice: x: 2, y: 2, z: 4, core: 2. Of those that a mesh axis runs over, the one named last changes fastest.
Arguments:
- hidden_in: bfloat16 [2048, 8192], P(('groups', 'ctx'), 'tp'), parts along dimension 0, may hold values from -20 to 20
- attn_gain: bfloat16 [8192], replicated, may hold values from 0.5 to 1.5
- query_weight: bfloat16 [8192, 4096], P(None, 'tp'), may hold values from -0.0625 to 0.0625
- keys: bfloat16 [16384, 512], P(('groups', 'ctx')), parts along dimension 0, may hold values from -300 to 300
- values: bfloat16 [16384, 512], P(('groups', 'ctx')), parts along dimension 0, may hold values from -6 to 6
- offset: int32 [2], P('groups'), parts along dimension 0, may hold values from 4096 to 7168
- out_weight: bfloat16 [4096, 8192], P('tp'), may hold values from -1 to 1
- sign_bits: int32 [8192], replicated, may hold values from 0 to 1
- attn_exps: int32 [64, 64], P(('groups', 'ctx')), parts along dimension 0, may hold values from -8 to -5
- norm_gain: bfloat16 [8192], replicated, may hold values from 0.25 to 1.75
- norm_exps: int32 [64, 64], P(('groups', 'ctx')), parts along dimension 0, may hold values from -6 to -4
Outputs:
- normed: bfloat16 [2048, 8192], P(('groups', 'ctx')), parts along dimension 0
There are 2 independent parts, one for each index of `groups`. A program takes and returns all parts, laid end to end along the dimension named above; an argument that names none is the same for every part. Nothing has to cross between parts.
Inputs may be any that keep to these rules, and one draw needn't show every extreme that they name: `offset`: every query row sees all of the first 4096 context positions.
All inputs are finite; a program needn't handle non-finite values.
Results may differ from a plain program's by a relative error of at most 0.014.
The roundings to bfloat16 on the way count: a program that leaves them out, or rounds other values in their place, can miss the bound.
Values may be sent and summed in bfloat16 or wider, within the bound.
No kernel may reach another device: no remote copies, remote signals or barrier semaphores. Data moves between devices by JAX's collectives and lax.ppermute only.
A program may use at most 256 MiB of HBM per device.

v0:
```python
import functools
import math

import jax
import jax.numpy as jnp
from jax import lax
from jax.experimental import pallas as pl
from jax.experimental.pallas import tpu as pltpu
from jax.sharding import PartitionSpec as P

HD = 128
KVH = 4
HB = 128
RB = 32
MIB = 1 << 20
EPS = 1e-05
LOG2E = math.log2(math.e)


def _params(mib, **kw):
    return pltpu.CompilerParams(vmem_limit_bytes=mib * MIB, **kw)


def _cost(flops, moved):
    return pl.CostEstimate(flops=flops // 20, bytes_accessed=moved // 20, transcendentals=0)


def _permute(value, axis, pairs):
    return lax.ppermute(value, axis, pairs)


def _both(value, axis, count):
    if count == 2:
        other = _permute(value, axis, [(0, 1), (1, 0)])
        first = lax.axis_index(axis) == 0
        return jnp.stack([jnp.where(first, value, other), jnp.where(first, other, value)])
    return lax.all_gather(value, axis, axis=0)


def _spread(blocks, places, axis, count):
    if count == 2:
        mate = [_permute(b, axis, [(0, 1), (1, 0)]) for b in blocks]
        return blocks + mate, [2 * p + lax.axis_index(axis) for p in places] + [
            2 * p + 1 - lax.axis_index(axis) for p in places
        ]
    whole = [lax.all_gather(b, axis, axis=0) for b in blocks]
    return [w[i] for w in whole for i in range(count)], [count * p + i for p in places for i in range(count)]


def _after(values, events):
    return list(lax.optimization_barrier((tuple(values), tuple(events)))[0])


class Line:
    def __init__(self, zc, yc):
        self.zc, self.yc, self.n = zc, yc, zc * yc
        self.z = lax.axis_index("tp") // yc
        self.y = lax.axis_index("tp") % yc

    def across(self, v):
        return _permute(v, "tp", [(s, s ^ 1) for s in range(self.n)])

    def up(self, v, k):
        zc, yc = self.zc, self.yc
        return _permute(v, "tp", [(s, s + yc) for s in range(self.n) if k - 1 <= s // yc < zc - 1])

    def down(self, v, k):
        zc, yc = self.zc, self.yc
        return _permute(v, "tp", [(s, s - yc) for s in range(self.n) if 1 <= s // yc <= zc - k])

    def pick(self, a, b, c, d):
        z = self.z
        return jnp.where(z == 0, a, jnp.where(z == 1, b, jnp.where(z == 2, c, d)))

    def ids(self):
        layers = [self.z, self.pick(1, 0, 1, 2), self.pick(2, 2, 3, 1), self.pick(3, 3, 0, 0)]
        y, yc = self.y, self.yc
        return jnp.stack([l * yc + y for l in layers] + [l * yc + (1 - y) for l in layers]).astype(jnp.int32)

    def gather(self, x):
        z, bar = self.z, lax.optimization_barrier
        d1, u1, y0 = bar((self.down(x, 1), self.up(x, 1), self.across(x)))
        va = jnp.where(z == 0, d1, u1)
        (va, u1, d1), _ = bar(((va, u1, d1), (yield y0)))
        d2, u2, ya = bar((self.down(d1, 2), self.up(u1, 2), self.across(va)))
        vb = jnp.where(z == 0, d2, jnp.where(z == 3, u2, d1))
        (vb, u2, d2), _ = bar(((vb, u2, d2), (yield ya)))
        d3, u3, yb = bar((self.down(d2, 3), self.up(u2, 3), self.across(vb)))
        vc = jnp.where(z == 0, d3, jnp.where(z == 1, d2, jnp.where(z == 2, u2, u3)))
        (vc,), _ = bar(((vc,), (yield yb)))
        yield [x, va, vb, vc, y0, ya, yb, self.across(vc)]


def gather_tp(value, zc, yc):
    if zc == 4 and yc == 2:
        line = Line(zc, yc)
        return line.gather(value), line.ids()
    n = zc * yc

    def steps():
        whole = lax.all_gather(value, "tp", axis=0)
        yield whole
        yield whole
        yield whole
        yield [whole[i] for i in range(n)]

    return steps(), jnp.arange(n, dtype=jnp.int32)


def _squares(parts):
    total = None
    for p in parts:
        for c in range(0, p.shape[1], 128):
            f = p[:, c : c + 128].astype(jnp.float32)
            total = f * f if total is None else total + f * f
    return jnp.sum(total, axis=1, keepdims=True)


def _query_kernel(n, heads, ids, *refs):
    parts = refs[:n]
    gain, weight, cos, sin, out = refs[n:]
    width = parts[0].shape[1]
    d = n * width
    r = lax.rsqrt(_squares([p[...] for p in parts]) / d + EPS)
    acc = None
    for i in range(n):
        at = ids[i]
        normed = (parts[i][...].astype(jnp.float32) * r * gain[at]).astype(jnp.bfloat16)
        rows = pl.ds(pl.multiple_of(at * width, width), width)
        t = jnp.dot(normed, weight[rows, :], preferred_element_type=jnp.float32)
        acc = t if acc is None else acc + t
    for h in range(heads):
        v = acc[:, h * HD : (h + 1) * HD]
        turned = v * cos[...] + pltpu.roll(v, HD // 2, 1) * sin[...]
        out[h] = turned.astype(jnp.bfloat16)


def project_queries(blocks, ids, gain, weight, cos, sin):
    n = len(blocks)
    rows, part = blocks[0].shape
    d, width = weight.shape
    heads = width // HD
    tile = min(256, rows)
    gains = gain.astype(jnp.float32).reshape(n, 1, part)
    grid_spec = pltpu.PrefetchScalarGridSpec(
        num_scalar_prefetch=1,
        grid=(rows // tile,),
        in_specs=[pl.BlockSpec((tile, part), lambda i, ids: (i, 0))] * n
        + [
            pl.BlockSpec((n, 1, part), lambda i, ids: (0, 0, 0)),
            pl.BlockSpec((d, width), lambda i, ids: (0, 0), pipeline_mode=pl.Buffered(1)),
            pl.BlockSpec((tile, HD), lambda i, ids: (i, 0)),
            pl.BlockSpec((tile, HD), lambda i, ids: (i, 0)),
        ],
        out_specs=pl.BlockSpec((heads, tile, HD), lambda i, ids: (0, i, 0)),
    )
    return pl.pallas_call(
        functools.partial(_query_kernel, n, heads),
        grid_spec=grid_spec,
        out_shape=jax.ShapeDtypeStruct((heads, rows, HD), jnp.bfloat16),
        compiler_params=_params(48),
        cost_estimate=_cost(2 * rows * d * width, 2 * (rows * d + d * width)),
        name="query_projection",
    )(ids, *blocks, gains, weight, cos, sin)


CK = 1024


def _attend_kernel(heads, tile, span, info, q_ref, k_ref, v_ref, out, s_ref, m_ref, l_ref, acc_ref):
    step = pl.program_id(0)
    scale = LOG2E / math.sqrt(HD)
    m = heads * tile
    q = q_ref[...].reshape(m, HD)
    first_pos = info[0] + step * tile
    row_pos = first_pos + lax.rem(lax.broadcasted_iota(jnp.int32, (m, CK), 0), tile)

    def scores(base, j, masked):
        keys = k_ref[pl.ds(pl.multiple_of(base + j * CK, CK), CK), :]
        s = lax.dot_general(q, keys, (((1,), (1,)), ((), ())), preferred_element_type=jnp.float32)
        if masked:
            col = base + j * CK + lax.broadcasted_iota(jnp.int32, (m, CK), 1)
            s = jnp.where(col <= row_pos, s, -1e30)
        s_ref[:, pl.ds(pl.multiple_of(j * CK, CK), CK)] = s
        top = m_ref[...]
        for c in range(CK // 128):
            top = jnp.maximum(top, s[:, c * 128 : (c + 1) * 128])
        m_ref[...] = top

    def weigh(base, j, top):
        s = s_ref[:, pl.ds(pl.multiple_of(j * CK, CK), CK)]
        p = jnp.exp2((s - top) * scale)
        total = l_ref[...]
        for c in range(CK // 128):
            total = total + p[:, c * 128 : (c + 1) * 128]
        l_ref[...] = total
        vals = v_ref[pl.ds(pl.multiple_of(base + j * CK, CK), CK), :]
        acc_ref[...] += jnp.dot(p.astype(jnp.bfloat16), vals, preferred_element_type=jnp.float32)

    def block(base, full, count):
        m_ref[...] = jnp.full(m_ref.shape, -1e30, jnp.float32)
        l_ref[...] = jnp.zeros(l_ref.shape, jnp.float32)
        acc_ref[...] = jnp.zeros(acc_ref.shape, jnp.float32)

        def loop(n, f):
            lax.fori_loop(0, n, lambda j, c: (f(j), c)[1], 0)

        loop(full, lambda j: scores(base, j, False))
        if count is not full:
            lax.fori_loop(full, count, lambda j, c: (scores(base, j, True), c)[1], 0)
        top = jnp.max(m_ref[...], axis=1, keepdims=True)
        loop(count, lambda j: weigh(base, j, top))
        return top, jnp.sum(l_ref[...], axis=1, keepdims=True), acc_ref[...]

    chunks = span // CK
    blocks = k_ref.shape[0] // span
    top, total, acc = block(0, chunks, chunks)
    for b in range(1, blocks):
        base = b * span
        full = jnp.clip((first_pos + 1 - base) // CK, 0, chunks)
        count = jnp.clip((first_pos + tile - 1 - base) // CK + 1, 0, chunks)
        top2, total2, acc2 = block(base, full, count)
        new = jnp.maximum(top, top2)
        f1 = jnp.exp2((top - new) * scale)
        f2 = jnp.exp2((top2 - new) * scale)
        acc = f1 * acc + f2 * acc2
        total = f1 * total + f2 * total2
        top = new
    res = (acc / total).astype(jnp.bfloat16)
    for h in range(heads):
        out[:, h * HD : (h + 1) * HD] = res[h * tile : (h + 1) * tile]


def attend(q, keys, values, start, span):
    heads, rows, _ = q.shape
    tile = min(1024 // heads, rows)
    m = heads * tile
    total = keys.shape[0]
    grid_spec = pltpu.PrefetchScalarGridSpec(
        num_scalar_prefetch=1,
        grid=(rows // tile,),
        in_specs=[
            pl.BlockSpec((heads, tile, HD), lambda i, info: (0, i, 0)),
            pl.BlockSpec((total, HD), lambda i, info: (0, 0), pipeline_mode=pl.Buffered(1)),
            pl.BlockSpec((total, HD), lambda i, info: (0, 0), pipeline_mode=pl.Buffered(1)),
        ],
        out_specs=pl.BlockSpec((tile, heads * HD), lambda i, info: (i, 0)),
        scratch_shapes=[
            pltpu.VMEM((m, span), jnp.float32),
            pltpu.VMEM((m, 128), jnp.float32),
            pltpu.VMEM((m, 128), jnp.float32),
            pltpu.VMEM((m, HD), jnp.float32),
        ],
    )
    return pl.pallas_call(
        functools.partial(_attend_kernel, heads, tile, span),
        grid_spec=grid_spec,
        out_shape=jax.ShapeDtypeStruct((rows, heads * HD), jnp.bfloat16),
        compiler_params=_params(48),
        cost_estimate=_cost(4 * heads * rows * total * HD, 4 * total * HD),
        name="attend",
    )(start, q, keys, values)


def _spin(x, table):
    hi = x.astype(jnp.bfloat16)
    lo = (x - hi.astype(jnp.float32)).astype(jnp.bfloat16)
    return jnp.dot(hi, table, preferred_element_type=jnp.float32) + jnp.dot(
        lo, table, preferred_element_type=jnp.float32
    )


def _spread_exps(exps, first, width):
    count = exps.shape[1]
    shape = (count, width)
    at = first + lax.broadcasted_iota(jnp.int32, shape, 1) // HB
    pick = jnp.where(lax.broadcasted_iota(jnp.int32, shape, 0) == at, 1.0, 0.0).astype(jnp.bfloat16)
    return jnp.dot(exps.astype(jnp.float32).astype(jnp.bfloat16), pick, preferred_element_type=jnp.float32)


def _signs(bits):
    return (2 * bits - 1).astype(jnp.float32)


def _by_row_block(x, scale):
    blocks = scale.shape[0]
    rows, cols = x.shape
    return (x.reshape(blocks, rows // blocks, cols) * scale[:, None, :]).reshape(rows, cols)


def _code_kernel(zc, pieces, first, blocks, info, *refs):
    atts = refs[:zc]
    own = refs[zc]
    far = refs[zc + 1 : zc + 1 + (zc - 1) * pieces]
    table, bits, exps, out = refs[zc + 1 + (zc - 1) * pieces :]
    tile = table.shape[0]
    sign = _signs(bits[...])
    column = (info[0] + pl.program_id(0)) * (tile // HB)
    scale = jnp.exp2(-_spread_exps(exps[first : first + blocks, :], column, tile)) * (1.0 / math.sqrt(HB))
    piece = far[0].shape[0]
    parts = []
    for k in range(zc):
        if k == 0:
            a, w = atts[0][...], own[...]
        else:
            a = jnp.concatenate(
                [atts[k][:, pl.ds(pl.multiple_of(info[2 + p] * piece, piece), piece)] for p in range(pieces)], axis=1
            )
            w = jnp.concatenate([f[...] for f in far[(k - 1) * pieces : k * pieces]], axis=0)
        parts.append(jnp.dot(a, w, preferred_element_type=jnp.float32) * sign)
    rows = parts[0].shape[0]
    spun = _spin(jnp.concatenate(parts, axis=0), table[...])
    total = None
    for k in range(zc):
        coded = jnp.clip(_by_row_block(spun[k * rows : (k + 1) * rows], scale), -127.0, 127.0)
        coded = coded.astype(jnp.bfloat16).astype(jnp.float32)
        total = coded if total is None else total + coded
    out[...] = total.astype(out.dtype)


def code_terms(atts, own, far, places, table, bits, exps, chunk, z, side, out_type):
    zc = len(atts)
    rows, depth = atts[0].shape
    piece, cols = far[0][0].shape
    pieces = len(far[0])
    width = cols // 2
    tile = table.shape[0]
    steps = width // tile
    blocks = rows // RB
    info = jnp.stack([z * (cols // tile) + side * steps, side * steps] + places).astype(jnp.int32)
    grid_spec = pltpu.PrefetchScalarGridSpec(
        num_scalar_prefetch=1,
        grid=(steps,),
        in_specs=[pl.BlockSpec((rows, depth), lambda j, info: (0, 0), pipeline_mode=pl.Buffered(1))] * zc
        + [pl.BlockSpec((depth, tile), lambda j, info: (0, info[0] + j))]
        + [pl.BlockSpec((piece, tile), lambda j, info: (0, info[1] + j))] * (pieces * len(far))
        + [
            pl.BlockSpec((tile, tile), lambda j, info: (0, 0)),
            pl.BlockSpec((1, tile), lambda j, info: (0, info[0] + j)),
            pl.BlockSpec(exps.shape, lambda j, info: (0, 0)),
        ],
        out_specs=pl.BlockSpec((rows, tile), lambda j, info: (0, j)),
    )
    return pl.pallas_call(
        functools.partial(_code_kernel, zc, pieces, chunk * blocks, blocks),
        grid_spec=grid_spec,
        out_shape=jax.ShapeDtypeStruct((rows, width), out_type),
        compiler_params=_params(48),
        cost_estimate=_cost(2 * zc * rows * width * (depth + 2 * tile), 2 * zc * depth * width),
        name="code_terms",
    )(info, *atts, own, *[f for fs in far for f in fs], table, bits, exps)


def _residual_kernel(first, blocks, info, mine, theirs, hidden, table, bits, exps, out):
    summed = mine[...] + theirs[...].astype(jnp.float32)
    tile = table.shape[0]
    width = summed.shape[1]
    scale = jnp.exp2(_spread_exps(exps[first : first + blocks, :], info[0] * (width // HB), width))
    scale = scale * (1.0 / math.sqrt(HB))
    sign = _signs(bits[...])
    for j in range(width // tile):
        at = slice(j * tile, (j + 1) * tile)
        spun = _spin(summed[:, at], table[...])
        projected = _by_row_block(spun, scale[:, at]) * sign[:, at]
        out[:, at] = (hidden[:, at].astype(jnp.float32) + projected).astype(jnp.bfloat16)


def add_residual(mine, theirs, hidden, table, bits, exps, chunk, tp):
    rows, width = mine.shape
    blocks = rows // RB
    grid_spec = pltpu.PrefetchScalarGridSpec(
        num_scalar_prefetch=1,
        grid=(1,),
        in_specs=[
            pl.BlockSpec((rows, width), lambda i, info: (0, 0)),
            pl.BlockSpec((rows, width), lambda i, info: (0, 0)),
            pl.BlockSpec((rows, width), lambda i, info: (chunk, 0)),
            pl.BlockSpec(table.shape, lambda i, info: (0, 0)),
            pl.BlockSpec((1, width), lambda i, info: (0, info[0])),
            pl.BlockSpec(exps.shape, lambda i, info: (0, 0)),
        ],
        out_specs=pl.BlockSpec((rows, width), lambda i, info: (0, 0)),
    )
    return pl.pallas_call(
        functools.partial(_residual_kernel, chunk * blocks, blocks),
        grid_spec=grid_spec,
        out_shape=jax.ShapeDtypeStruct((rows, width), jnp.bfloat16),
        compiler_params=_params(48),
        cost_estimate=_cost(4 * rows * width * table.shape[0], 10 * rows * width),
        name="residual",
    )(tp.astype(jnp.int32).reshape(1), mine, theirs, hidden, table, bits, exps)


def _norm_kernel(n, ids, *refs):
    parts = refs[:n]
    gain, exps, out = refs[n], refs[n + 1], refs[-1]
    rows, width = parts[0].shape
    d = n * width
    r = lax.rsqrt(_squares([p[...] for p in parts]) / d + EPS)
    blocks = exps.shape[1]
    for i in range(n):
        at = ids[i]
        columns = pl.ds(pl.multiple_of(at * width, width), width)
        e = _spread_exps(exps[0], at * (width // HB), width)
        scaled = parts[i][...].astype(jnp.float32) * r
        g = gain[:, columns].astype(jnp.float32) * jnp.exp2(-e)
        code = jnp.clip(_by_row_block(scaled, g), -127.0, 127.0).astype(jnp.bfloat16)
        value = code.reshape(blocks, rows // blocks, width) * jnp.exp2(e).astype(jnp.bfloat16)[:, None, :]
        out[:, columns] = value.reshape(rows, width)


def norm_rows(blocks, ids, gain, exps, done, chunk, whole):
    n = len(blocks)
    rows, part = blocks[0].shape
    d = n * part
    tile = 128
    steps = rows // tile
    rb = tile // RB
    earlier = [] if done is None else [done]
    grid_spec = pltpu.PrefetchScalarGridSpec(
        num_scalar_prefetch=1,
        grid=(steps,),
        in_specs=[pl.BlockSpec((tile, part), lambda i, ids: (i, 0))] * n
        + [
            pl.BlockSpec((1, d), lambda i, ids: (0, 0)),
            pl.BlockSpec((1, rb, exps.shape[1]), lambda i, ids: (chunk * steps + i, 0, 0)),
        ]
        + [pl.BlockSpec(memory_space=pl.ANY)] * len(earlier),
        out_specs=pl.BlockSpec((tile, d), lambda i, ids: (chunk * steps + i, 0)),
    )
    return pl.pallas_call(
        functools.partial(_norm_kernel, n),
        grid_spec=grid_spec,
        out_shape=jax.ShapeDtypeStruct((whole, d), jnp.bfloat16),
        input_output_aliases={n + 3: 0} if earlier else {},
        compiler_params=_params(60),
        cost_estimate=_cost(8 * rows * d, 4 * rows * d),
        name="norm",
    )(ids, *blocks, gain, exps.reshape(-1, rb, exps.shape[1]), *earlier)


def hadamard_table(order):
    table = jnp.ones((1, 1), dtype=jnp.float32)
    while table.shape[0] < order:
        upper = jnp.concatenate([table, table], axis=1)
        lower = jnp.concatenate([table, -table], axis=1)
        table = jnp.concatenate([upper, lower], axis=0)
    return table


def rotary_tables(positions):
    half = HD // 2
    inv_freq = jnp.exp(-(jnp.arange(half, dtype=jnp.float32) * (2.0 / HD)) * math.log(500000.0))
    angles = positions.astype(jnp.float32)[:, None] * inv_freq[None, :]
    cos, sin = jnp.cos(angles), jnp.sin(angles)
    return jnp.concatenate([cos, cos], axis=1), jnp.concatenate([-sin, sin], axis=1)


def local(
    hidden_in,
    attn_gain,
    query_weight,
    keys,
    values,
    offset,
    out_weight,
    sign_bits,
    attn_exps,
    norm_gain,
    norm_exps,
):
    n_tp, csz, gsz = lax.axis_size("tp"), lax.axis_size("ctx"), lax.axis_size("groups")
    yc = 2 if n_tp % 2 == 0 else 1
    zc = n_tp // yc
    tp, ctx, grp = lax.axis_index("tp"), lax.axis_index("ctx"), lax.axis_index("groups")
    z, y = tp // yc, tp % yc
    rows, width = hidden_in.shape
    d = width * n_tp
    heads = query_weight.shape[1] // HD
    all_heads = heads * n_tp
    depth = out_weight.shape[0]
    cols = d // zc

    column = tp * heads // (all_heads // KVH) * HD
    own_keys = lax.dynamic_slice_in_dim(keys, column, HD, 1)
    own_values = lax.dynamic_slice_in_dim(values, column, HD, 1)
    span = keys.shape[0]
    all_keys = _both(own_keys, "ctx", csz).reshape(csz * span, HD)
    all_values = _both(own_values, "ctx", csz).reshape(csz * span, HD)

    size = rows // 2
    blocks_per = size // RB
    halves = [slice(0, size), slice(size, rows)]
    start = (offset[0] + ctx * rows).astype(jnp.int32)
    cos, sin = rotary_tables(start + jnp.arange(rows, dtype=jnp.int32))

    mine, shares = out_weight, []
    for axis, count, index in (("groups", gsz, grp), ("ctx", csz, ctx)):
        piece = mine.shape[0] // count
        if piece % 128 == 0:
            mine = lax.dynamic_slice_in_dim(mine, index * piece, piece, 0)
            shares.append((axis, count))
    steps = list(range(1, zc))
    batches = [steps[1::3], steps[2::3], steps[0::3]]
    moved, far = {}, {}

    def move(batch, *event):
        pieces = [lax.dynamic_slice_in_dim(mine, (z + k) % zc * cols, cols, 1) for k in batch]
        for k, piece in zip(batch, _after(pieces, event)):
            moved[k] = _permute(piece, "tp", [(s, (s + k * yc) % n_tp) for s in range(n_tp)])
            far[k] = [moved[k]], [jnp.int32(0)]

    def share(batch, level, *event):
        if level < len(shares):
            for k in batch:
                arrays, places = far[k]
                far[k] = _spread(_after(arrays, event), places, *shares[level])

    def arrived(batch):
        return [a for k in batch for a in far[k][0]]

    g0, ids = gather_tp(hidden_in[halves[0]], zc, yc)
    a1 = next(g0)
    g1, _ = gather_tp(_after([hidden_in[halves[1]]], [a1])[0], zc, yc)
    a2 = g0.send(a1)
    b1 = next(g1)
    a3 = g0.send(a2)
    b2 = g1.send(b1)
    move(batches[0], a3, b2)
    first = g0.send(a3)
    b3 = g1.send(b2)
    event = [b3] + arrived(batches[0])
    move(batches[1], *event)
    share(batches[0], 0, *event)
    second = g1.send(event)

    def queries_of(c, blocks):
        return project_queries(blocks, ids, attn_gain, query_weight, cos[halves[c]], sin[halves[c]])

    def heard_by(c, q):
        own = attend(q, all_keys, all_values, (start + c * size).reshape(1), span)
        return [own] + [_permute(own, "tp", [(s, (s + k * yc) % n_tp) for s in range(n_tp)]) for k in range(1, zc)]

    q = queries_of(0, first)
    move(batches[2], q)
    heard = [heard_by(0, q)]
    done = heard[0][0]
    share(batches[1], 0, done)
    share(batches[0], 1, done)
    q = queries_of(1, _after(second, [done]))
    share(batches[2], 0, q)
    heard.append(heard_by(1, q))
    done = heard[1][0]
    share(batches[1], 1, done)
    share(batches[2], 1, done)
    heard[0] = _after(heard[0], [done])
    places = far[1][1]
    far = [far[k][0] for k in steps]

    tile = 2 * HB
    h = hadamard_table(HB)
    zero = jnp.zeros_like(h)
    table = jnp.concatenate([jnp.concatenate([h, zero], 1), jnp.concatenate([zero, h], 1)], 0).astype(jnp.bfloat16)
    bits = sign_bits.reshape(1, d)

    def code_half(c, side, out_type):
        return code_terms(heard[c], out_weight, far, places, table, bits, attn_exps, c, z, side, out_type)

    def residual_of(c, sent, mine_sum):
        theirs = _permute(sent, "tp", [(s, s ^ 1) for s in range(n_tp)])
        return add_residual(mine_sum, theirs, hidden_in, table, bits, attn_exps, c, tp)

    residual = residual_of(0, code_half(0, 1 - y, jnp.bfloat16), code_half(0, y, jnp.float32))
    g0, ids = gather_tp(residual, zc, yc)
    a1 = next(g0)
    heard[1] = _after(heard[1], [residual])
    sent = code_half(1, 1 - y, jnp.bfloat16)
    heard[1] = _after(heard[1], [sent, residual])
    residual = residual_of(1, sent, code_half(1, y, jnp.float32))

    g1, _ = gather_tp(_after([residual], [a1])[0], zc, yc)
    a2 = g0.send(a1)
    b1 = next(g1)
    a3 = g0.send(a2)
    b2 = g1.send(b1)
    first = g0.send(a3)
    b3 = g1.send(b2)
    second = g1.send(b3)
    norm_row = norm_gain.reshape(1, d)
    out = norm_rows(first, ids, norm_row, norm_exps, None, 0, rows)
    return norm_rows(second, ids, norm_row, norm_exps, out, 1, rows)


def solution(mesh):
    return jax.shard_map(
        local,
        mesh=mesh,
        in_specs=(
            P(("groups", "ctx"), "tp"),
            P(),
            P(None, "tp"),
            P(("groups", "ctx"), None),
            P(("groups", "ctx"), None),
            P("groups"),
            P("tp", None),
            P(),
            P(("groups", "ctx"), None),
            P(),
            P(("groups", "ctx"), None),
        ),
        out_specs=P(("groups", "ctx"), None),
        check_vma=False,
    )
```

profile of v0, /device:TPU:0, one launch (start us, length us, event | category | flops | bytes accessed | tf_op | source)
XLA Modules:
  0.0 315.5 jit_solution(15628471964165656970)
XLA Ops:
  1.3 3.0 collective-permute-start.2
  4.3 4.3 %collective-permute-start.1 = (bf16[256,1024]{1,0:T(8,128)(2,1)S(1)}, bf16[256,1024]{1,0:T(8,128)(2,1)}, u32[]{:S(2)}, u32[]{:S(2)}) collective-permute-start(bf16[256,1024]{1,0:T(8,128)(2,1)S(1)} %get-tuple-element.208.refs_0_), channel_id=1, source_target_pairs={{0,2},{1,3},{2,4},{3,5},{4,6},{5,7},{8,10},{9,11},{10,12},{11,13},... | collective-permute-start | bytes 1572872 | tf_op jit(solution)/shard_map/ppermute | solution.py:29
  9.9 2.3 constant_dynamic-slice_fusion
  12.9 2.3 constant_dynamic-slice_fusion.1
  16.3 2.4 collective-permute-done.1
  18.7 4.9 %collective-permute-done = bf16[256,1024]{1,0:T(8,128)(2,1)S(1)} collective-permute-done((bf16[256,1024]{1,0:T(8,128)(2,1)S(1)}, bf16[256,1024]{1,0:T(8,128)(2,1)S(1)}, u32[]{:S(2)}, u32[]{:S(2)}) %collective-permute-start) | collective-permute-done | bytes 524320 | tf_op jit(solution)/shard_map/ppermute | solution.py:29
  26.3 1.8 multiply_sine_fusion
  28.2 1.3 pad_maximum_fusion.3
  30.6 1.6 collective-permute-start.5
  32.2 8.7 %collective-permute-start.4 = (bf16[256,1024]{1,0:T(8,128)(2,1)S(1)}, bf16[256,1024]{1,0:T(8,128)(2,1)S(1)}, u32[]{:S(2)}, u32[]{:S(2)}) collective-permute-start(bf16[256,1024]{1,0:T(8,128)(2,1)S(1)} %get-tuple-element.137.refs_0_), channel_id=1, source_target_pairs={{0,2},{1,3},{2,4},{3,5},{4,6},{5,7},{8,10},{9,11},{10,12},{11,13},... | collective-permute-start | bytes 1572872 | tf_op jit(solution)/shard_map/ppermute | solution.py:29
  42.5 3.3 %fusion.3 = (bf16[128,2048]{1,0:T(8,128)(2,1)}, bf16[128,2048]{1,0:T(8,128)(2,1)}, bf16[128,2048]{1,0:T(8,128)(2,1)S(1)}) fusion(bf16[512,8192]{1,0:T(8,128)(2,1)} %refs_4_.7, s32[]{:T(128)S(6)} %dynamic_slice.22, s32[]{:T(128)S(6)} %select_n.270, s32[]{:T(128)S(6)} %select_n.267, s32[]{:T(128)S(6)} %select_n.251), kind=kLoop, calls=%fused_computation.33 | loop fusion | bytes 3145744 | tf_op jit(solution)/shard_map/dynamic_slice | solution.py:508
  47.2 2.0 collective-permute-done.5.refs_4_
  51.2 3.9 %collective-permute-done.3 = bf16[256,1024]{1,0:T(8,128)(2,1)S(1)} collective-permute-done((bf16[256,1024]{1,0:T(8,128)(2,1)S(1)}, bf16[256,1024]{1,0:T(8,128)(2,1)S(1)}, u32[]{:S(2)}, u32[]{:S(2)}) %collective-permute-start.3) | collective-permute-done | bytes 524320 | tf_op jit(solution)/shard_map/ppermute | solution.py:29
  56.4 2.0 select_bitcast_fusion.1
  58.4 1.6 collective-permute-start.8
  60.0 5.7 %collective-permute-done.15 = bf16[256,1024]{1,0:T(8,128)(2,1)S(1)} collective-permute-done((bf16[256,1024]{1,0:T(8,128)(2,1)}, bf16[256,1024]{1,0:T(8,128)(2,1)S(1)}, u32[]{:S(2)}, u32[]{:S(2)}) %collective-permute-start.15) | collective-permute-done | bytes 524320 | tf_op jit(solution)/shard_map/ppermute | solution.py:29
  66.9 1.6 select_bitcast_fusion.3
  68.6 1.4 collective-permute-done.17.refs_6_
  70.0 6.0 %collective-permute-done.8.refs_5_ = bf16[256,1024]{1,0:T(8,128)(2,1)S(1)} collective-permute-done((bf16[256,1024]{1,0:T(8,128)(2,1)S(1)}, bf16[256,1024]{1,0:T(8,128)(2,1)S(1)}, u32[]{:S(2)}, u32[]{:S(2)}) %collective-permute-start.8) | collective-permute-done | bytes 524320 | tf_op jit(solution)/shard_map/ppermute | solution.py:29
  76.0 2.7 collective-permute-done.6
  81.4 2.8 collective-permute-start.18
  84.3 1.6 collective-permute-start.20
  86.0 7.7 %collective-permute-done.11.refs_6_ = bf16[256,1024]{1,0:T(8,128)(2,1)S(1)} collective-permute-done((bf16[256,1024]{1,0:T(8,128)(2,1)S(1)}, bf16[256,1024]{1,0:T(8,128)(2,1)S(1)}, u32[]{:S(2)}, u32[]{:S(2)}) %collective-permute-start.11) | collective-permute-done | bytes 524320 | tf_op jit(solution)/shard_map/ppermute | solution.py:29
  93.7 9.8 %collective-permute-done.18.refs_9_ = bf16[128,2048]{1,0:T(8,128)(2,1)S(1)} collective-permute-done((bf16[128,2048]{1,0:T(8,128)(2,1)S(1)}, bf16[128,2048]{1,0:T(8,128)(2,1)S(1)}, u32[]{:S(2)}, u32[]{:S(2)}) %collective-permute-start.18) | collective-permute-done | bytes 524320 | tf_op jit(solution)/shard_map/ppermute | solution.py:29
  103.5 2.1 collective-permute-start.36
  105.8 7.3 %query_projection.2.q_ref = bf16[4,256,128]{2,1,0:T(8,128)(2,1)S(1)} custom-call(s32[8]{0:T(128)S(1)} %stack.110.ids, bf16[256,1024]{1,0:T(8,128)(2,1)S(1)} %copy-done.16, bf16[256,1024]{1,0:T(8,128)(2,1)S(1)} %copy-done.12, bf16[256,1024]{1,0:T(8,128)(2,1)S(1)} %select_select_fusion.5.refs_2_, bf16[256,1024]{1,0:T(8,128)(2,1)S(1)} %select_select_fusion.4.refs_3_, ...), custom_call_target="tpu_custom_call" | custom-call | flops 107374184 | bytes 629145 | tf_op jit(solution)/shard_map/query_projection/pallas_call | solution.py:157
  113.1 1.6 collective-permute-start.19
  114.7 1.5 collective-permute-start.33
  116.4 9.0 %attend.2.refs_0_ = bf16[256,512]{1,0:T(8,128)(2,1)S(1)} custom-call(s32[1]{0:T(128)} %bitcast.17.info, bf16[4,256,128]{2,1,0:T(8,128)(2,1)S(1)} %query_projection.2.q_ref, bf16[8192,128]{1,0:T(8,128)(2,1)S(1)} %bitcast.36, bf16[8192,128]{1,0:T(8,128)(2,1)S(1)} %bitcast.34), custom_call_target="tpu_custom_call" | custom-call | flops 214748368 | bytes 209715 | tf_op jit(solution)/shard_map/attend/pallas_call | solution.py:255
  126.8 3.6 %collective-permute-start.37 = (bf16[128,2048]{1,0:T(8,128)(2,1)S(1)}, bf16[128,2048]{1,0:T(8,128)(2,1)}, u32[]{:S(2)}, u32[]{:S(2)}) collective-permute-start(bf16[128,2048]{1,0:T(8,128)(2,1)S(1)} %collective-permute-done.36.refs_13_), channel_id=1, source_target_pairs={{0,16},{16,0},{1,17},{17,1},{2,18},{18,2},{3,19},{19,3},{4,20},{20... | collective-permute-start | bytes 1572872 | tf_op jit(solution)/shard_map/ppermute | solution.py:29
  130.4 7.3 %query_projection.3.q_ref = bf16[4,256,128]{2,1,0:T(8,128)(2,1)S(1)} custom-call(s32[8]{0:T(128)S(1)} %stack.110.ids, bf16[256,1024]{1,0:T(8,128)(2,1)S(1)} %copy-done.14, bf16[256,1024]{1,0:T(8,128)(2,1)S(1)} %broadcast_select_fusion.3.refs_1_, bf16[256,1024]{1,0:T(8,128)(2,1)S(1)} %select_select_fusion.7.refs_2_, ...), custom_call_target="tpu_custom_call" | custom-call | flops 107374184 | bytes 629145 | tf_op jit(solution)/shard_map/query_projection/pallas_call | solution.py:157
  138.5 3.9 %collective-permute-start.28 = (bf16[256,512]{1,0:T(8,128)(2,1)S(1)}, bf16[256,512]{1,0:T(8,128)(2,1)}, u32[]{:S(2)}, u32[]{:S(2)}) collective-permute-start(bf16[256,512]{1,0:T(8,128)(2,1)S(1)} %attend.2.refs_0_), channel_id=1, source_target_pairs={{0,6},{1,7},{2,0},{3,1},{4,2},{5,3},{6,4},{7,5},{8,14},{9,15},{10,... | collective-permute-start | bytes 786440 | tf_op jit(solution)/shard_map/ppermute | solution.py:29
  143.2 1.6 copy-done.1
  145.8 9.1 %attend.3.refs_0_ = bf16[256,512]{1,0:T(8,128)(2,1)S(1)} custom-call(s32[1]{0:T(128)} %bitcast.16.info, bf16[4,256,128]{2,1,0:T(8,128)(2,1)S(1)} %copy-done.22, bf16[8192,128]{1,0:T(8,128)(2,1)S(1)} %bitcast.37, bf16[8192,128]{1,0:T(8,128)(2,1)S(1)} %bitcast.35), custom_call_target="tpu_custom_call" | custom-call | flops 214748368 | bytes 209715 | tf_op jit(solution)/shard_map/attend/pallas_call | solution.py:255
  156.8 6.8 %collective-permute-done.27.refs_2_ = bf16[256,512]{1,0:T(8,128)(2,1)} collective-permute-done((bf16[256,512]{1,0:T(8,128)(2,1)S(1)}, bf16[256,512]{1,0:T(8,128)(2,1)}, u32[]{:S(2)}, u32[]{:S(2)}) %collective-permute-start.27) | collective-permute-done | bytes 262176 | tf_op jit(solution)/shard_map/ppermute | solution.py:29
  164.3 2.2 collective-permute-done.39.refs_16_
  168.0 6.4 %code_terms.5 = bf16[256,1024]{1,0:T(8,128)(2,1)} custom-call(s32[6]{0:T(128)S(1)} %stack.126.info, bf16[256,512]{1,0:T(8,128)(2,1)S(1)} %attend.2.refs_0_, bf16[256,512]{1,0:T(8,128)(2,1)} %collective-permute-done.26.refs_1_, bf16[256,512]{1,0:T(8,128)(2,1)} %collective-permute-done.27.refs_2_, bf16[256,512]{1,0:T(8,128)(2,1)} %collective-permute-done.28.refs_3_, ...), custom_call_target="tpu_custom_call" | custom-call | flops 107374184 | bytes 209715 | tf_op jit(solution)/shard_map/code_terms/pallas_call | solution.py:344
  175.2 3.4 %collective-permute-start.24 = (bf16[256,512]{1,0:T(8,128)(2,1)S(1)}, bf16[256,512]{1,0:T(8,128)(2,1)}, u32[]{:S(2)}, u32[]{:S(2)}) collective-permute-start(bf16[256,512]{1,0:T(8,128)(2,1)S(1)} %copy-done.10), channel_id=1, source_target_pairs={{0,4},{1,5},{2,6},{3,7},{4,0},{5,1},{6,2},{7,3},{8,12},{9,13},{10,... | collective-permute-start | bytes 786440 | tf_op jit(solution)/shard_map/ppermute | solution.py:29
  178.6 2.0 collective-permute-start.23
  180.7 6.4 %code_terms.4.mine = f32[256,1024]{1,0:T(8,128)} custom-call(s32[6]{0:T(128)S(1)} %stack.117.info, bf16[256,512]{1,0:T(8,128)(2,1)S(1)} %attend.2.refs_0_, bf16[256,512]{1,0:T(8,128)(2,1)} %collective-permute-done.26.refs_1_, bf16[256,512]{1,0:T(8,128)(2,1)} %collective-permute-done.27.refs_2_, bf16[256,512]{1,0:T(8,128)(2,1)} %collective-permute-done.28.refs_3_, ...), custom_call_target="tpu_custom_call" | custom-call | flops 107374184 | bytes 209715 | tf_op jit(solution)/shard_map/code_terms/pallas_call | solution.py:344
  187.1 1.5 collective-permute-done.40.theirs
  189.9 1.6 residual.2.refs_0_
  192.1 3.6 %collective-permute-start.43 = (bf16[256,1024]{1,0:T(8,128)(2,1)S(1)}, bf16[256,1024]{1,0:T(8,128)(2,1)S(1)}, u32[]{:S(2)}, u32[]{:S(2)}) collective-permute-start(bf16[256,1024]{1,0:T(8,128)(2,1)S(1)} %residual.2.refs_0_), channel_id=1, source_target_pairs={{0,2},{1,3},{2,4},{3,5},{4,6},{5,7},{8,10},{9,11},{10,12},{11,13},... | collective-permute-start | bytes 1572872 | tf_op jit(solution)/shard_map/ppermute | solution.py:29
  197.0 5.6 %collective-permute-done.24.refs_2_ = bf16[256,512]{1,0:T(8,128)(2,1)} collective-permute-done((bf16[256,512]{1,0:T(8,128)(2,1)S(1)}, bf16[256,512]{1,0:T(8,128)(2,1)}, u32[]{:S(2)}, u32[]{:S(2)}) %collective-permute-start.24) | collective-permute-done | bytes 262176 | tf_op jit(solution)/shard_map/ppermute | solution.py:29
  202.5 5.9 %code_terms.6 = bf16[256,1024]{1,0:T(8,128)(2,1)S(1)} custom-call(s32[6]{0:T(128)S(1)} %stack.126.info, bf16[256,512]{1,0:T(8,128)(2,1)S(1)} %copy-done.10, bf16[256,512]{1,0:T(8,128)(2,1)} %collective-permute-done.23.refs_1_, bf16[256,512]{1,0:T(8,128)(2,1)} %collective-permute-done.24.refs_2_, bf16[256,512]{1,0:T(8,128)(2,1)} %collective-permute-done.25.refs_3_, ...), custom_call_target="tpu_custom_call" | custom-call | flops 107374184 | bytes 209715 | tf_op jit(solution)/shard_map/code_terms/pallas_call | solution.py:344
  208.4 1.7 collective-permute-start.41
  210.1 6.4 %code_terms.7.mine = f32[256,1024]{1,0:T(8,128)} custom-call(s32[6]{0:T(128)S(1)} %stack.117.info, bf16[256,512]{1,0:T(8,128)(2,1)S(1)} %copy-done.10, bf16[256,512]{1,0:T(8,128)(2,1)} %collective-permute-done.23.refs_1_, bf16[256,512]{1,0:T(8,128)(2,1)} %collective-permute-done.24.refs_2_, bf16[256,512]{1,0:T(8,128)(2,1)} %collective-permute-done.25.refs_3_, ...), custom_call_target="tpu_custom_call" | custom-call | flops 107374184 | bytes 209715 | tf_op jit(solution)/shard_map/code_terms/pallas_call | solution.py:344
  216.6 4.3 %collective-permute-done.41.theirs = bf16[256,1024]{1,0:T(8,128)(2,1)S(1)} collective-permute-done((bf16[256,1024]{1,0:T(8,128)(2,1)S(1)}, bf16[256,1024]{1,0:T(8,128)(2,1)S(1)}, u32[]{:S(2)}, u32[]{:S(2)}) %collective-permute-start.41) | collective-permute-done | bytes 524320 | tf_op jit(solution)/shard_map/ppermute | solution.py:29
  222.7 1.6 collective-permute-start.47
  224.2 1.3 collective-permute-start.46
  228.2 9.4 %collective-permute-done.47.refs_4_ = bf16[256,1024]{1,0:T(8,128)(2,1)S(1)} collective-permute-done((bf16[256,1024]{1,0:T(8,128)(2,1)S(1)}, bf16[256,1024]{1,0:T(8,128)(2,1)S(1)}, u32[]{:S(2)}, u32[]{:S(2)}) %collective-permute-start.47) | collective-permute-done | bytes 524320 | tf_op jit(solution)/shard_map/ppermute | solution.py:29
  238.9 2.7 collective-permute-done.45
  243.8 5.1 %collective-permute-done.57.refs_5_ = bf16[256,1024]{1,0:T(8,128)(2,1)S(1)} collective-permute-done((bf16[256,1024]{1,0:T(8,128)(2,1)S(1)}, bf16[256,1024]{1,0:T(8,128)(2,1)S(1)}, u32[]{:S(2)}, u32[]{:S(2)}) %collective-permute-start.57) | collective-permute-done | bytes 524320 | tf_op jit(solution)/shard_map/ppermute | solution.py:29
  248.8 3.9 %collective-permute-done.55 = bf16[256,1024]{1,0:T(8,128)(2,1)S(1)} collective-permute-done((bf16[256,1024]{1,0:T(8,128)(2,1)S(1)}, bf16[256,1024]{1,0:T(8,128)(2,1)S(1)}, u32[]{:S(2)}, u32[]{:S(2)}) %collective-permute-start.55) | collective-permute-done | bytes 524320 | tf_op jit(solution)/shard_map/ppermute | solution.py:29
  255.4 4.6 %collective-permute-done.50.refs_5_ = bf16[256,1024]{1,0:T(8,128)(2,1)S(1)} collective-permute-done((bf16[256,1024]{1,0:T(8,128)(2,1)S(1)}, bf16[256,1024]{1,0:T(8,128)(2,1)S(1)}, u32[]{:S(2)}, u32[]{:S(2)}) %collective-permute-start.50) | collective-permute-done | bytes 524320 | tf_op jit(solution)/shard_map/ppermute | solution.py:29
  260.1 5.0 %collective-permute-done.48 = bf16[256,1024]{1,0:T(8,128)(2,1)S(1)} collective-permute-done((bf16[256,1024]{1,0:T(8,128)(2,1)S(1)}, bf16[256,1024]{1,0:T(8,128)(2,1)S(1)}, u32[]{:S(2)}, u32[]{:S(2)}) %collective-permute-start.48) | collective-permute-done | bytes 524320 | tf_op jit(solution)/shard_map/ppermute | solution.py:29
  267.0 4.3 %collective-permute-done.60.refs_6_ = bf16[256,1024]{1,0:T(8,128)(2,1)S(1)} collective-permute-done((bf16[256,1024]{1,0:T(8,128)(2,1)S(1)}, bf16[256,1024]{1,0:T(8,128)(2,1)S(1)}, u32[]{:S(2)}, u32[]{:S(2)}) %collective-permute-start.60) | collective-permute-done | bytes 524320 | tf_op jit(solution)/shard_map/ppermute | solution.py:29
  272.2 4.0 %collective-permute-done.58 = bf16[256,1024]{1,0:T(8,128)(2,1)S(1)} collective-permute-done((bf16[256,1024]{1,0:T(8,128)(2,1)S(1)}, bf16[256,1024]{1,0:T(8,128)(2,1)S(1)}, u32[]{:S(2)}, u32[]{:S(2)}) %collective-permute-start.58) | collective-permute-done | bytes 524320 | tf_op jit(solution)/shard_map/ppermute | solution.py:29
  276.3 2.9 collective-permute-done.53.refs_6_
  279.2 4.3 %collective-permute-done.51 = bf16[256,1024]{1,0:T(8,128)(2,1)S(1)} collective-permute-done((bf16[256,1024]{1,0:T(8,128)(2,1)S(1)}, bf16[256,1024]{1,0:T(8,128)(2,1)S(1)}, u32[]{:S(2)}, u32[]{:S(2)}) %collective-permute-start.51) | collective-permute-done | bytes 524320 | tf_op jit(solution)/shard_map/ppermute | solution.py:29
  284.5 1.4 collective-permute-start.54
  286.5 12.2 %collective-permute-done.61.refs_7_ = bf16[256,1024]{1,0:T(8,128)(2,1)S(1)} collective-permute-done((bf16[256,1024]{1,0:T(8,128)(2,1)S(1)}, bf16[256,1024]{1,0:T(8,128)(2,1)S(1)}, u32[]{:S(2)}, u32[]{:S(2)}) %collective-permute-start.61) | collective-permute-done | bytes 524320 | tf_op jit(solution)/shard_map/ppermute | solution.py:29
  299.5 7.5 %norm.2.refs_10_ = bf16[512,8192]{1,0:T(8,128)(2,1)} custom-call(s32[8]{0:T(128)} %copy-done.30, bf16[256,1024]{1,0:T(8,128)(2,1)} %copy-done.17, bf16[256,1024]{1,0:T(8,128)(2,1)} %copy-done.34, bf16[256,1024]{1,0:T(8,128)(2,1)} %copy-done.36, bf16[256,1024]{1,0:T(8,128)(2,1)} %copy-done.33, bf16[256,1024]{1,0:T(8,128)(2,1)} %copy-done.39, ...), custom_call_target="tpu_custom_call" | custom-call | flops 838860 | bytes 419430 | tf_op jit(solution)/shard_map/norm/pallas_call | solution.py:431
  307.9 7.5 %norm.3 = bf16[512,8192]{1,0:T(8,128)(2,1)} custom-call(s32[8]{0:T(128)} %copy-done.30, bf16[256,1024]{1,0:T(8,128)(2,1)} %copy-done.18, bf16[256,1024]{1,0:T(8,128)(2,1)} %copy-done.35, bf16[256,1024]{1,0:T(8,128)(2,1)} %copy-done.37, bf16[256,1024]{1,0:T(8,128)(2,1)} %copy-done.32, bf16[256,1024]{1,0:T(8,128)(2,1)} %copy-done.40, ...), custom_call_target="tpu_custom_call", output_to_operand_aliasing={{}: (11, {})} | custom-call | flops 838860 | bytes 419430 | tf_op jit(solution)/shard_map/norm/pallas_call | solution.py:431
  (201 shorter events, 46.9 us)
Async XLA Ops:
  1.3 15.0 %collective-permute-start.2 = (bf16[256,1024]{1,0:T(8,128)(2,1)S(1)}, bf16[256,1024]{1,0:T(8,128)(2,1)S(1)}, u32[]{:S(2)}, u32[]{:S(2)}) collective-permute-start(bf16[256,1024]{1,0:T(8,128)(2,1)S(1)} %get-tuple-element.208.refs_0_), channel_id=1, source_target_pairs={{0,1},{1,0},{2,3},{3,2},{4,5},{5,4},{6,7},{7,6},{8,9},{9,8},{10,11... | collective-permute-start | bytes 1572872 | tf_op jit(solution)/shard_map/ppermute | solution.py:29
  4.3 14.4 %collective-permute-start.1 = (bf16[256,1024]{1,0:T(8,128)(2,1)S(1)}, bf16[256,1024]{1,0:T(8,128)(2,1)}, u32[]{:S(2)}, u32[]{:S(2)}) collective-permute-start(bf16[256,1024]{1,0:T(8,128)(2,1)S(1)} %get-tuple-element.208.refs_0_), channel_id=1, source_target_pairs={{0,2},{1,3},{2,4},{3,5},{4,6},{5,7},{8,10},{9,11},{10,12},{11,13},... | collective-permute-start | bytes 1572872 | tf_op jit(solution)/shard_map/ppermute | solution.py:29
  8.6 15.0 %collective-permute-start = (bf16[256,1024]{1,0:T(8,128)(2,1)S(1)}, bf16[256,1024]{1,0:T(8,128)(2,1)S(1)}, u32[]{:S(2)}, u32[]{:S(2)}) collective-permute-start(bf16[256,1024]{1,0:T(8,128)(2,1)S(1)} %get-tuple-element.208.refs_0_), channel_id=1, source_target_pairs={{2,0},{3,1},{4,2},{5,3},{6,4},{7,5},{10,8},{11,9},{12,10},{13,11},... | collective-permute-start | bytes 1572872 | tf_op jit(solution)/shard_map/ppermute | solution.py:29
  12.2 43.5 %collective-permute-start.22 = (bf16[4096,128]{1,0:T(8,128)(2,1)}, bf16[4096,128]{1,0:T(8,128)(2,1)}, u32[]{:S(2)}, u32[]{:S(2)}) collective-permute-start(bf16[4096,128]{1,0:T(8,128)(2,1)} %constant_dynamic-slice_fusion), channel_id=1, source_target_pairs={{0,8},{8,0},{1,9},{9,1},{2,10},{10,2},{3,11},{11,3},{4,12},{12,4},... | collective-permute-start | bytes 3145736 | tf_op jit(solution)/shard_map/ppermute | solution.py:29
  23.7 8.5 %collective-permute-start.13 = (bf16[256,1024]{1,0:T(8,128)(2,1)}, bf16[256,1024]{1,0:T(8,128)(2,1)S(1)}, u32[]{:S(2)}, u32[]{:S(2)}) collective-permute-start(bf16[256,1024]{1,0:T(8,128)(2,1)} %collective-permute-done.1), channel_id=1, source_target_pairs={{2,4},{3,5},{4,6},{5,7},{10,12},{11,13},{12,14},{13,15},{18,20},{1... | collective-permute-start | bytes 1572872 | tf_op jit(solution)/shard_map/ppermute | solution.py:29
  24.4 16.8 %collective-permute-start.12 = (bf16[256,1024]{1,0:T(8,128)(2,1)S(1)}, bf16[256,1024]{1,0:T(8,128)(2,1)}, u32[]{:S(2)}, u32[]{:S(2)}) collective-permute-start(bf16[256,1024]{1,0:T(8,128)(2,1)S(1)} %collective-permute-done), channel_id=1, source_target_pairs={{2,0},{3,1},{4,2},{5,3},{10,8},{11,9},{12,10},{13,11},{18,16},{19,... | collective-permute-start | bytes 1572872 | tf_op jit(solution)/shard_map/ppermute | solution.py:29
  25.7 20.1 %collective-permute-start.14 = (bf16[256,1024]{1,0:T(8,128)(2,1)S(1)}, bf16[256,1024]{1,0:T(8,128)(2,1)S(1)}, u32[]{:S(2)}, u32[]{:S(2)}) collective-permute-start(bf16[256,1024]{1,0:T(8,128)(2,1)S(1)} %broadcast_select_fusion.2.refs_1_), channel_id=1, source_target_pairs={{0,1},{1,0},{2,3},{3,2},{4,5},{5,4},{6,7},{7,6},{8,9},{9,8},{10,11... | collective-permute-start | bytes 1572872 | tf_op jit(solution)/shard_map/ppermute | solution.py:29
  28.1 77.7 %copy-start.28 = (f32[8192]{0:T(1024)}, f32[8192]{0:T(1024)S(1)}, u32[]{:S(2)}) copy-start(f32[8192]{0:T(1024)S(1)} %reshape.54) | copy-start | bytes 98308
  28.2 102.2 %copy-start.30 = (s32[8]{0:T(128)}, s32[8]{0:T(128)S(1)}, u32[]{:S(2)}) copy-start(s32[8]{0:T(128)S(1)} %stack.110.ids) | copy-start | bytes 100
  30.6 18.5 %collective-permute-start.5 = (bf16[256,1024]{1,0:T(8,128)(2,1)S(1)}, bf16[256,1024]{1,0:T(8,128)(2,1)S(1)}, u32[]{:S(2)}, u32[]{:S(2)}) collective-permute-start(bf16[256,1024]{1,0:T(8,128)(2,1)S(1)} %get-tuple-element.137.refs_0_), channel_id=1, source_target_pairs={{0,1},{1,0},{2,3},{3,2},{4,5},{5,4},{6,7},{7,6},{8,9},{9,8},{10,11... | collective-permute-start | bytes 1572872 | tf_op jit(solution)/shard_map/ppermute | solution.py:29
  32.2 18.3 %collective-permute-start.4 = (bf16[256,1024]{1,0:T(8,128)(2,1)S(1)}, bf16[256,1024]{1,0:T(8,128)(2,1)S(1)}, u32[]{:S(2)}, u32[]{:S(2)}) collective-permute-start(bf16[256,1024]{1,0:T(8,128)(2,1)S(1)} %get-tuple-element.137.refs_0_), channel_id=1, source_target_pairs={{0,2},{1,3},{2,4},{3,5},{4,6},{5,7},{8,10},{9,11},{10,12},{11,13},... | collective-permute-start | bytes 1572872 | tf_op jit(solution)/shard_map/ppermute | solution.py:29
  41.2 13.9 %collective-permute-start.3 = (bf16[256,1024]{1,0:T(8,128)(2,1)S(1)}, bf16[256,1024]{1,0:T(8,128)(2,1)S(1)}, u32[]{:S(2)}, u32[]{:S(2)}) collective-permute-start(bf16[256,1024]{1,0:T(8,128)(2,1)S(1)} %get-tuple-element.137.refs_0_), channel_id=1, source_target_pairs={{2,0},{3,1},{4,2},{5,3},{6,4},{7,5},{10,8},{11,9},{12,10},{13,11},... | collective-permute-start | bytes 1572872 | tf_op jit(solution)/shard_map/ppermute | solution.py:29
  45.8 12.5 %collective-permute-start.21 = (bf16[4096,128]{1,0:T(8,128)(2,1)S(1)}, bf16[4096,128]{1,0:T(8,128)(2,1)S(1)}, u32[]{:S(2)}, u32[]{:S(2)}) collective-permute-start(bf16[4096,128]{1,0:T(8,128)(2,1)S(1)} %copy-done.38), channel_id=1, source_target_pairs={{0,8},{8,0},{1,9},{9,1},{2,10},{10,2},{3,11},{11,3},{4,12},{12,4},... | collective-permute-start | bytes 3145736 | tf_op jit(solution)/shard_map/ppermute | solution.py:29
  49.2 16.5 %collective-permute-start.15 = (bf16[256,1024]{1,0:T(8,128)(2,1)}, bf16[256,1024]{1,0:T(8,128)(2,1)S(1)}, u32[]{:S(2)}, u32[]{:S(2)}) collective-permute-start(bf16[256,1024]{1,0:T(8,128)(2,1)} %collective-permute-done.12), channel_id=1, source_target_pairs={{2,0},{3,1},{10,8},{11,9},{18,16},{19,17},{26,24},{27,25}} | collective-permute-start | bytes 1572872 | tf_op jit(solution)/shard_map/ppermute | solution.py:29
  50.5 18.1 %collective-permute-start.16 = (bf16[256,1024]{1,0:T(8,128)(2,1)S(1)}, bf16[256,1024]{1,0:T(8,128)(2,1)S(1)}, u32[]{:S(2)}, u32[]{:S(2)}) collective-permute-start(bf16[256,1024]{1,0:T(8,128)(2,1)S(1)} %collective-permute-done.13), channel_id=1, source_target_pairs={{4,6},{5,7},{12,14},{13,15},{20,22},{21,23},{28,30},{29,31}} | collective-permute-start | bytes 1572872 | tf_op jit(solution)/shard_map/ppermute | solution.py:29
  55.1 14.9 %collective-permute-start.17 = (bf16[256,1024]{1,0:T(8,128)(2,1)S(1)}, bf16[256,1024]{1,0:T(8,128)(2,1)S(1)}, u32[]{:S(2)}, u32[]{:S(2)}) collective-permute-start(bf16[256,1024]{1,0:T(8,128)(2,1)S(1)} %select_select_fusion.5.refs_2_), channel_id=1, source_target_pairs={{0,1},{1,0},{2,3},{3,2},{4,5},{5,4},{6,7},{7,6},{8,9},{9,8},{10,11... | collective-permute-start | bytes 1572872 | tf_op jit(solution)/shard_map/ppermute | solution.py:29
  55.7 14.3 %collective-permute-start.7 = (bf16[256,1024]{1,0:T(8,128)(2,1)S(1)}, bf16[256,1024]{1,0:T(8,128)(2,1)S(1)}, u32[]{:S(2)}, u32[]{:S(2)}) collective-permute-start(bf16[256,1024]{1,0:T(8,128)(2,1)S(1)} %collective-permute-done.4), channel_id=1, source_target_pairs={{2,4},{3,5},{4,6},{5,7},{10,12},{11,13},{12,14},{13,15},{18,20},{1... | collective-permute-start | bytes 1572872 | tf_op jit(solution)/shard_map/ppermute | solution.py:29
  58.4 17.6 %collective-permute-start.8 = (bf16[256,1024]{1,0:T(8,128)(2,1)S(1)}, bf16[256,1024]{1,0:T(8,128)(2,1)S(1)}, u32[]{:S(2)}, u32[]{:S(2)}) collective-permute-start(bf16[256,1024]{1,0:T(8,128)(2,1)S(1)} %broadcast_select_fusion.3.refs_1_), channel_id=1, source_target_pairs={{0,1},{1,0},{2,3},{3,2},{4,5},{5,4},{6,7},{7,6},{8,9},{9,8},{10,11... | collective-permute-start | bytes 1572872 | tf_op jit(solution)/shard_map/ppermute | solution.py:29
  65.7 13.0 %collective-permute-start.6 = (bf16[256,1024]{1,0:T(8,128)(2,1)S(1)}, bf16[256,1024]{1,0:T(8,128)(2,1)S(1)}, u32[]{:S(2)}, u32[]{:S(2)}) collective-permute-start(bf16[256,1024]{1,0:T(8,128)(2,1)S(1)} %collective-permute-done.3), channel_id=1, source_target_pairs={{2,0},{3,1},{4,2},{5,3},{10,8},{11,9},{12,10},{13,11},{18,16},{19,... | collective-permute-start | bytes 1572872 | tf_op jit(solution)/shard_map/ppermute | solution.py:29
  78.8 14.9 %collective-permute-start.11 = (bf16[256,1024]{1,0:T(8,128)(2,1)S(1)}, bf16[256,1024]{1,0:T(8,128)(2,1)S(1)}, u32[]{:S(2)}, u32[]{:S(2)}) collective-permute-start(bf16[256,1024]{1,0:T(8,128)(2,1)S(1)} %select_select_fusion.7.refs_2_), channel_id=1, source_target_pairs={{0,1},{1,0},{2,3},{3,2},{4,5},{5,4},{6,7},{7,6},{8,9},{9,8},{10,11... | collective-permute-start | bytes 1572872 | tf_op jit(solution)/shard_map/ppermute | solution.py:29
  79.3 14.4 %collective-permute-start.9 = (bf16[256,1024]{1,0:T(8,128)(2,1)S(1)}, bf16[256,1024]{1,0:T(8,128)(2,1)S(1)}, u32[]{:S(2)}, u32[]{:S(2)}) collective-permute-start(bf16[256,1024]{1,0:T(8,128)(2,1)S(1)} %collective-permute-done.6), channel_id=1, source_target_pairs={{2,0},{3,1},{10,8},{11,9},{18,16},{19,17},{26,24},{27,25}} | collective-permute-start | bytes 1572872 | tf_op jit(solution)/shard_map/ppermute | solution.py:29
  80.6 13.1 %collective-permute-start.10 = (bf16[256,1024]{1,0:T(8,128)(2,1)S(1)}, bf16[256,1024]{1,0:T(8,128)(2,1)S(1)}, u32[]{:S(2)}, u32[]{:S(2)}) collective-permute-start(bf16[256,1024]{1,0:T(8,128)(2,1)S(1)} %collective-permute-done.7), channel_id=1, source_target_pairs={{4,6},{5,7},{12,14},{13,15},{20,22},{21,23},{28,30},{29,31}} | collective-permute-start | bytes 1572872 | tf_op jit(solution)/shard_map/ppermute | solution.py:29
  81.4 22.2 %collective-permute-start.18 = (bf16[128,2048]{1,0:T(8,128)(2,1)S(1)}, bf16[128,2048]{1,0:T(8,128)(2,1)S(1)}, u32[]{:S(2)}, u32[]{:S(2)}) collective-permute-start(bf16[128,2048]{1,0:T(8,128)(2,1)S(1)} %get-tuple-element.132), channel_id=1, source_target_pairs={{0,4},{1,5},{2,6},{3,7},{4,0},{5,1},{6,2},{7,3},{8,12},{9,13},{10,... | collective-permute-start | bytes 1572872 | tf_op jit(solution)/shard_map/ppermute | solution.py:29
  84.3 21.5 %collective-permute-start.20 = (bf16[256,1024]{1,0:T(8,128)(2,1)S(1)}, bf16[256,1024]{1,0:T(8,128)(2,1)S(1)}, u32[]{:S(2)}, u32[]{:S(2)}) collective-permute-start(bf16[256,1024]{1,0:T(8,128)(2,1)S(1)} %select_select_fusion.4.refs_3_), channel_id=1, source_target_pairs={{0,1},{1,0},{2,3},{3,2},{4,5},{5,4},{6,7},{7,6},{8,9},{9,8},{10,11... | collective-permute-start | bytes 1572872 | tf_op jit(solution)/shard_map/ppermute | solution.py:29
  103.5 23.2 %collective-permute-start.36 = (bf16[128,2048]{1,0:T(8,128)(2,1)}, bf16[128,2048]{1,0:T(8,128)(2,1)S(1)}, u32[]{:S(2)}, u32[]{:S(2)}) collective-permute-start(bf16[128,2048]{1,0:T(8,128)(2,1)} %get-tuple-element.156), channel_id=1, source_target_pairs={{0,6},{1,7},{2,0},{3,1},{4,2},{5,3},{6,4},{7,5},{8,14},{9,15},{10,... | collective-permute-start | bytes 1572872 | tf_op jit(solution)/shard_map/ppermute | solution.py:29
  113.1 17.3 %collective-permute-start.19 = (bf16[256,1024]{1,0:T(8,128)(2,1)S(1)}, bf16[256,1024]{1,0:T(8,128)(2,1)S(1)}, u32[]{:S(2)}, u32[]{:S(2)}) collective-permute-start(bf16[256,1024]{1,0:T(8,128)(2,1)S(1)} %select_select_fusion.6.refs_3_), channel_id=1, source_target_pairs={{0,1},{1,0},{2,3},{3,2},{4,5},{5,4},{6,7},{7,6},{8,9},{9,8},{10,11... | collective-permute-start | bytes 1572872 | tf_op jit(solution)/shard_map/ppermute | solution.py:29
  114.7 23.8 %collective-permute-start.33 = (bf16[128,2048]{1,0:T(8,128)(2,1)S(1)}, bf16[128,2048]{1,0:T(8,128)(2,1)}, u32[]{:S(2)}, u32[]{:S(2)}) collective-permute-start(bf16[128,2048]{1,0:T(8,128)(2,1)S(1)} %collective-permute-done.18.refs_9_), channel_id=1, source_target_pairs={{0,16},{16,0},{1,17},{17,1},{2,18},{18,2},{3,19},{19,3},{4,20},{20... | collective-permute-start | bytes 1572872 | tf_op jit(solution)/shard_map/ppermute | solution.py:29
  116.2 22.2 %collective-permute-start.29 = (bf16[128,2048]{1,0:T(8,128)(2,1)S(1)}, bf16[128,2048]{1,0:T(8,128)(2,1)}, u32[]{:S(2)}, u32[]{:S(2)}) collective-permute-start(bf16[128,2048]{1,0:T(8,128)(2,1)S(1)} %copy-done.47), channel_id=1, source_target_pairs={{0,2},{1,3},{2,4},{3,5},{4,6},{5,7},{6,0},{7,1},{8,10},{9,11},{10,... | collective-permute-start | bytes 1572872 | tf_op jit(solution)/shard_map/ppermute | solution.py:29
  126.8 16.5 %collective-permute-start.37 = (bf16[128,2048]{1,0:T(8,128)(2,1)S(1)}, bf16[128,2048]{1,0:T(8,128)(2,1)}, u32[]{:S(2)}, u32[]{:S(2)}) collective-permute-start(bf16[128,2048]{1,0:T(8,128)(2,1)S(1)} %collective-permute-done.36.refs_13_), channel_id=1, source_target_pairs={{0,16},{16,0},{1,17},{17,1},{2,18},{18,2},{3,19},{19,3},{4,20},{20... | collective-permute-start | bytes 1572872 | tf_op jit(solution)/shard_map/ppermute | solution.py:29
  138.4 17.2 %collective-permute-start.30 = (bf16[128,2048]{1,0:T(8,128)(2,1)}, bf16[128,2048]{1,0:T(8,128)(2,1)}, u32[]{:S(2)}, u32[]{:S(2)}) collective-permute-start(bf16[128,2048]{1,0:T(8,128)(2,1)} %collective-permute-done.29.refs_5_), channel_id=1, source_target_pairs={{0,16},{16,0},{1,17},{17,1},{2,18},{18,2},{3,19},{19,3},{4,20},{20... | collective-permute-start | bytes 1572872 | tf_op jit(solution)/shard_map/ppermute | solution.py:29
  138.4 25.7 %collective-permute-start.34 = (bf16[128,2048]{1,0:T(8,128)(2,1)S(1)}, bf16[128,2048]{1,0:T(8,128)(2,1)}, u32[]{:S(2)}, u32[]{:S(2)}) collective-permute-start(bf16[128,2048]{1,0:T(8,128)(2,1)S(1)} %collective-permute-done.18.refs_9_), channel_id=1, source_target_pairs={{0,8},{8,0},{1,9},{9,1},{2,10},{10,2},{3,11},{11,3},{4,12},{12,4},... | collective-permute-start | bytes 1572872 | tf_op jit(solution)/shard_map/ppermute | solution.py:29
  138.5 18.2 %collective-permute-start.28 = (bf16[256,512]{1,0:T(8,128)(2,1)S(1)}, bf16[256,512]{1,0:T(8,128)(2,1)}, u32[]{:S(2)}, u32[]{:S(2)}) collective-permute-start(bf16[256,512]{1,0:T(8,128)(2,1)S(1)} %attend.2.refs_0_), channel_id=1, source_target_pairs={{0,6},{1,7},{2,0},{3,1},{4,2},{5,3},{6,4},{7,5},{8,14},{9,15},{10,... | collective-permute-start | bytes 786440 | tf_op jit(solution)/shard_map/ppermute | solution.py:29
  142.4 21.2 %collective-permute-start.27 = (bf16[256,512]{1,0:T(8,128)(2,1)S(1)}, bf16[256,512]{1,0:T(8,128)(2,1)}, u32[]{:S(2)}, u32[]{:S(2)}) collective-permute-start(bf16[256,512]{1,0:T(8,128)(2,1)S(1)} %attend.2.refs_0_), channel_id=1, source_target_pairs={{0,4},{1,5},{2,6},{3,7},{4,0},{5,1},{6,2},{7,3},{8,12},{9,13},{10,... | collective-permute-start | bytes 786440 | tf_op jit(solution)/shard_map/ppermute | solution.py:29
  143.2 20.4 %collective-permute-start.26 = (bf16[256,512]{1,0:T(8,128)(2,1)S(1)}, bf16[256,512]{1,0:T(8,128)(2,1)}, u32[]{:S(2)}, u32[]{:S(2)}) collective-permute-start(bf16[256,512]{1,0:T(8,128)(2,1)S(1)} %attend.2.refs_0_), channel_id=1, source_target_pairs={{0,2},{1,3},{2,4},{3,5},{4,6},{5,7},{6,0},{7,1},{8,10},{9,11},{10,... | collective-permute-start | bytes 786440 | tf_op jit(solution)/shard_map/ppermute | solution.py:29
  155.6 8.7 %collective-permute-start.35 = (bf16[128,2048]{1,0:T(8,128)(2,1)}, bf16[128,2048]{1,0:T(8,128)(2,1)S(1)}, u32[]{:S(2)}, u32[]{:S(2)}) collective-permute-start(bf16[128,2048]{1,0:T(8,128)(2,1)} %collective-permute-done.33.refs_10_), channel_id=1, source_target_pairs={{0,8},{8,0},{1,9},{9,1},{2,10},{10,2},{3,11},{11,3},{4,12},{12,4},... | collective-permute-start | bytes 1572872 | tf_op jit(solution)/shard_map/ppermute | solution.py:29
  156.7 7.5 %collective-permute-start.38 = (bf16[128,2048]{1,0:T(8,128)(2,1)S(1)}, bf16[128,2048]{1,0:T(8,128)(2,1)S(1)}, u32[]{:S(2)}, u32[]{:S(2)}) collective-permute-start(bf16[128,2048]{1,0:T(8,128)(2,1)S(1)} %collective-permute-done.36.refs_13_), channel_id=1, source_target_pairs={{0,8},{8,0},{1,9},{9,1},{2,10},{10,2},{3,11},{11,3},{4,12},{12,4},... | collective-permute-start | bytes 1572872 | tf_op jit(solution)/shard_map/ppermute | solution.py:29
  163.6 2.9 collective-permute-start.39
  163.6 2.9 collective-permute-start.31
  164.1 3.1 collective-permute-start.32
  174.4 14.3 %collective-permute-start.40 = (bf16[256,1024]{1,0:T(8,128)(2,1)}, bf16[256,1024]{1,0:T(8,128)(2,1)}, u32[]{:S(2)}, u32[]{:S(2)}) collective-permute-start(bf16[256,1024]{1,0:T(8,128)(2,1)} %code_terms.5), channel_id=1, source_target_pairs={{0,1},{1,0},{2,3},{3,2},{4,5},{5,4},{6,7},{7,6},{8,9},{9,8},{10,11... | collective-permute-start | bytes 1572872 | tf_op jit(solution)/shard_map/ppermute | solution.py:29
  174.9 20.7 %collective-permute-start.25 = (bf16[256,512]{1,0:T(8,128)(2,1)S(1)}, bf16[256,512]{1,0:T(8,128)(2,1)}, u32[]{:S(2)}, u32[]{:S(2)}) collective-permute-start(bf16[256,512]{1,0:T(8,128)(2,1)S(1)} %copy-done.10), channel_id=1, source_target_pairs={{0,6},{1,7},{2,0},{3,1},{4,2},{5,3},{6,4},{7,5},{8,14},{9,15},{10,... | collective-permute-start | bytes 786440 | tf_op jit(solution)/shard_map/ppermute | solution.py:29
  175.2 27.4 %collective-permute-start.24 = (bf16[256,512]{1,0:T(8,128)(2,1)S(1)}, bf16[256,512]{1,0:T(8,128)(2,1)}, u32[]{:S(2)}, u32[]{:S(2)}) collective-permute-start(bf16[256,512]{1,0:T(8,128)(2,1)S(1)} %copy-done.10), channel_id=1, source_target_pairs={{0,4},{1,5},{2,6},{3,7},{4,0},{5,1},{6,2},{7,3},{8,12},{9,13},{10,... | collective-permute-start | bytes 786440 | tf_op jit(solution)/shard_map/ppermute | solution.py:29
  178.6 24.0 %collective-permute-start.23 = (bf16[256,512]{1,0:T(8,128)(2,1)S(1)}, bf16[256,512]{1,0:T(8,128)(2,1)}, u32[]{:S(2)}, u32[]{:S(2)}) collective-permute-start(bf16[256,512]{1,0:T(8,128)(2,1)S(1)} %copy-done.10), channel_id=1, source_target_pairs={{0,2},{1,3},{2,4},{3,5},{4,6},{5,7},{6,0},{7,1},{8,10},{9,11},{10,... | collective-permute-start | bytes 786440 | tf_op jit(solution)/shard_map/ppermute | solution.py:29
  191.5 25.1 %collective-permute-start.44 = (bf16[256,1024]{1,0:T(8,128)(2,1)S(1)}, bf16[256,1024]{1,0:T(8,128)(2,1)S(1)}, u32[]{:S(2)}, u32[]{:S(2)}) collective-permute-start(bf16[256,1024]{1,0:T(8,128)(2,1)S(1)} %residual.2.refs_0_), channel_id=1, source_target_pairs={{0,1},{1,0},{2,3},{3,2},{4,5},{5,4},{6,7},{7,6},{8,9},{9,8},{10,11... | collective-permute-start | bytes 1572872 | tf_op jit(solution)/shard_map/ppermute | solution.py:29
  192.1 24.5 %collective-permute-start.43 = (bf16[256,1024]{1,0:T(8,128)(2,1)S(1)}, bf16[256,1024]{1,0:T(8,128)(2,1)S(1)}, u32[]{:S(2)}, u32[]{:S(2)}) collective-permute-start(bf16[256,1024]{1,0:T(8,128)(2,1)S(1)} %residual.2.refs_0_), channel_id=1, source_target_pairs={{0,2},{1,3},{2,4},{3,5},{4,6},{5,7},{8,10},{9,11},{10,12},{11,13},... | collective-permute-start | bytes 1572872 | tf_op jit(solution)/shard_map/ppermute | solution.py:29
  195.7 20.9 %collective-permute-start.42 = (bf16[256,1024]{1,0:T(8,128)(2,1)S(1)}, bf16[256,1024]{1,0:T(8,128)(2,1)S(1)}, u32[]{:S(2)}, u32[]{:S(2)}) collective-permute-start(bf16[256,1024]{1,0:T(8,128)(2,1)S(1)} %residual.2.refs_0_), channel_id=1, source_target_pairs={{2,0},{3,1},{4,2},{5,3},{6,4},{7,5},{10,8},{11,9},{12,10},{13,11},... | collective-permute-start | bytes 1572872 | tf_op jit(solution)/shard_map/ppermute | solution.py:29
  208.4 12.5 %collective-permute-start.41 = (bf16[256,1024]{1,0:T(8,128)(2,1)S(1)}, bf16[256,1024]{1,0:T(8,128)(2,1)S(1)}, u32[]{:S(2)}, u32[]{:S(2)}) collective-permute-start(bf16[256,1024]{1,0:T(8,128)(2,1)S(1)} %code_terms.6), channel_id=1, source_target_pairs={{0,1},{1,0},{2,3},{3,2},{4,5},{5,4},{6,7},{7,6},{8,9},{9,8},{10,11... | collective-permute-start | bytes 1572872 | tf_op jit(solution)/shard_map/ppermute | solution.py:29
  222.7 14.9 %collective-permute-start.47 = (bf16[256,1024]{1,0:T(8,128)(2,1)S(1)}, bf16[256,1024]{1,0:T(8,128)(2,1)S(1)}, u32[]{:S(2)}, u32[]{:S(2)}) collective-permute-start(bf16[256,1024]{1,0:T(8,128)(2,1)S(1)} %residual.3.refs_0_), channel_id=1, source_target_pairs={{0,1},{1,0},{2,3},{3,2},{4,5},{5,4},{6,7},{7,6},{8,9},{9,8},{10,11... | collective-permute-start | bytes 1572872 | tf_op jit(solution)/shard_map/ppermute | solution.py:29
  224.2 14.6 %collective-permute-start.46 = (bf16[256,1024]{1,0:T(8,128)(2,1)S(1)}, bf16[256,1024]{1,0:T(8,128)(2,1)S(1)}, u32[]{:S(2)}, u32[]{:S(2)}) collective-permute-start(bf16[256,1024]{1,0:T(8,128)(2,1)S(1)} %residual.3.refs_0_), channel_id=1, source_target_pairs={{0,2},{1,3},{2,4},{3,5},{4,6},{5,7},{8,10},{9,11},{10,12},{11,13},... | collective-permute-start | bytes 1572872 | tf_op jit(solution)/shard_map/ppermute | solution.py:29
  225.6 16.0 %collective-permute-start.45 = (bf16[256,1024]{1,0:T(8,128)(2,1)S(1)}, bf16[256,1024]{1,0:T(8,128)(2,1)S(1)}, u32[]{:S(2)}, u32[]{:S(2)}) collective-permute-start(bf16[256,1024]{1,0:T(8,128)(2,1)S(1)} %residual.3.refs_0_), channel_id=1, source_target_pairs={{2,0},{3,1},{4,2},{5,3},{6,4},{7,5},{10,8},{11,9},{12,10},{13,11},... | collective-permute-start | bytes 1572872 | tf_op jit(solution)/shard_map/ppermute | solution.py:29
  226.9 15.5 %collective-permute-start.56 = (bf16[256,1024]{1,0:T(8,128)(2,1)S(1)}, bf16[256,1024]{1,0:T(8,128)(2,1)S(1)}, u32[]{:S(2)}, u32[]{:S(2)}) collective-permute-start(bf16[256,1024]{1,0:T(8,128)(2,1)S(1)} %collective-permute-done.43), channel_id=1, source_target_pairs={{2,4},{3,5},{4,6},{5,7},{10,12},{11,13},{12,14},{13,15},{18,20},{1... | collective-permute-start | bytes 1572872 | tf_op jit(solution)/shard_map/ppermute | solution.py:29
  227.6 21.2 %collective-permute-start.57 = (bf16[256,1024]{1,0:T(8,128)(2,1)S(1)}, bf16[256,1024]{1,0:T(8,128)(2,1)S(1)}, u32[]{:S(2)}, u32[]{:S(2)}) collective-permute-start(bf16[256,1024]{1,0:T(8,128)(2,1)S(1)} %broadcast_select_fusion.refs_1_), channel_id=1, source_target_pairs={{0,1},{1,0},{2,3},{3,2},{4,5},{5,4},{6,7},{7,6},{8,9},{9,8},{10,11... | collective-permute-start | bytes 1572872 | tf_op jit(solution)/shard_map/ppermute | solution.py:29
  237.6 15.2 %collective-permute-start.55 = (bf16[256,1024]{1,0:T(8,128)(2,1)S(1)}, bf16[256,1024]{1,0:T(8,128)(2,1)S(1)}, u32[]{:S(2)}, u32[]{:S(2)}) collective-permute-start(bf16[256,1024]{1,0:T(8,128)(2,1)S(1)} %collective-permute-done.42), channel_id=1, source_target_pairs={{2,0},{3,1},{4,2},{5,3},{10,8},{11,9},{12,10},{13,11},{18,16},{19,... | collective-permute-start | bytes 1572872 | tf_op jit(solution)/shard_map/ppermute | solution.py:29
  241.6 13.1 %collective-permute-start.49 = (bf16[256,1024]{1,0:T(8,128)(2,1)S(1)}, bf16[256,1024]{1,0:T(8,128)(2,1)S(1)}, u32[]{:S(2)}, u32[]{:S(2)}) collective-permute-start(bf16[256,1024]{1,0:T(8,128)(2,1)S(1)} %collective-permute-done.46), channel_id=1, source_target_pairs={{2,4},{3,5},{4,6},{5,7},{10,12},{11,13},{12,14},{13,15},{18,20},{1... | collective-permute-start | bytes 1572872 | tf_op jit(solution)/shard_map/ppermute | solution.py:29
  242.3 17.7 %collective-permute-start.50 = (bf16[256,1024]{1,0:T(8,128)(2,1)S(1)}, bf16[256,1024]{1,0:T(8,128)(2,1)S(1)}, u32[]{:S(2)}, u32[]{:S(2)}) collective-permute-start(bf16[256,1024]{1,0:T(8,128)(2,1)S(1)} %broadcast_select_fusion.1.refs_1_), channel_id=1, source_target_pairs={{0,1},{1,0},{2,3},{3,2},{4,5},{5,4},{6,7},{7,6},{8,9},{9,8},{10,11... | collective-permute-start | bytes 1572872 | tf_op jit(solution)/shard_map/ppermute | solution.py:29
  242.5 22.6 %collective-permute-start.48 = (bf16[256,1024]{1,0:T(8,128)(2,1)S(1)}, bf16[256,1024]{1,0:T(8,128)(2,1)S(1)}, u32[]{:S(2)}, u32[]{:S(2)}) collective-permute-start(bf16[256,1024]{1,0:T(8,128)(2,1)S(1)} %collective-permute-done.45), channel_id=1, source_target_pairs={{2,0},{3,1},{4,2},{5,3},{10,8},{11,9},{12,10},{13,11},{18,16},{19,... | collective-permute-start | bytes 1572872 | tf_op jit(solution)/shard_map/ppermute | solution.py:29
  252.9 18.4 %collective-permute-start.60 = (bf16[256,1024]{1,0:T(8,128)(2,1)S(1)}, bf16[256,1024]{1,0:T(8,128)(2,1)S(1)}, u32[]{:S(2)}, u32[]{:S(2)}) collective-permute-start(bf16[256,1024]{1,0:T(8,128)(2,1)S(1)} %select_select_fusion.1.refs_2_), channel_id=1, source_target_pairs={{0,1},{1,0},{2,3},{3,2},{4,5},{5,4},{6,7},{7,6},{8,9},{9,8},{10,11... | collective-permute-start | bytes 1572872 | tf_op jit(solution)/shard_map/ppermute | solution.py:29
  253.4 22.9 %collective-permute-start.58 = (bf16[256,1024]{1,0:T(8,128)(2,1)S(1)}, bf16[256,1024]{1,0:T(8,128)(2,1)S(1)}, u32[]{:S(2)}, u32[]{:S(2)}) collective-permute-start(bf16[256,1024]{1,0:T(8,128)(2,1)S(1)} %collective-permute-done.55), channel_id=1, source_target_pairs={{2,0},{3,1},{10,8},{11,9},{18,16},{19,17},{26,24},{27,25}} | collective-permute-start | bytes 1572872 | tf_op jit(solution)/shard_map/ppermute | solution.py:29
  254.7 21.6 %collective-permute-start.59 = (bf16[256,1024]{1,0:T(8,128)(2,1)S(1)}, bf16[256,1024]{1,0:T(8,128)(2,1)S(1)}, u32[]{:S(2)}, u32[]{:S(2)}) collective-permute-start(bf16[256,1024]{1,0:T(8,128)(2,1)S(1)} %collective-permute-done.56), channel_id=1, source_target_pairs={{4,6},{5,7},{12,14},{13,15},{20,22},{21,23},{28,30},{29,31}} | collective-permute-start | bytes 1572872 | tf_op jit(solution)/shard_map/ppermute | solution.py:29
  265.1 14.0 %collective-permute-start.53 = (bf16[256,1024]{1,0:T(8,128)(2,1)S(1)}, bf16[256,1024]{1,0:T(8,128)(2,1)S(1)}, u32[]{:S(2)}, u32[]{:S(2)}) collective-permute-start(bf16[256,1024]{1,0:T(8,128)(2,1)S(1)} %select_select_fusion.3.refs_2_), channel_id=1, source_target_pairs={{0,1},{1,0},{2,3},{3,2},{4,5},{5,4},{6,7},{7,6},{8,9},{9,8},{10,11... | collective-permute-start | bytes 1572872 | tf_op jit(solution)/shard_map/ppermute | solution.py:29
  265.7 17.7 %collective-permute-start.51 = (bf16[256,1024]{1,0:T(8,128)(2,1)S(1)}, bf16[256,1024]{1,0:T(8,128)(2,1)S(1)}, u32[]{:S(2)}, u32[]{:S(2)}) collective-permute-start(bf16[256,1024]{1,0:T(8,128)(2,1)S(1)} %collective-permute-done.48), channel_id=1, source_target_pairs={{2,0},{3,1},{10,8},{11,9},{18,16},{19,17},{26,24},{27,25}} | collective-permute-start | bytes 1572872 | tf_op jit(solution)/shard_map/ppermute | solution.py:29
  271.3 12.2 %collective-permute-start.52 = (bf16[256,1024]{1,0:T(8,128)(2,1)S(1)}, bf16[256,1024]{1,0:T(8,128)(2,1)S(1)}, u32[]{:S(2)}, u32[]{:S(2)}) collective-permute-start(bf16[256,1024]{1,0:T(8,128)(2,1)S(1)} %collective-permute-done.49), channel_id=1, source_target_pairs={{4,6},{5,7},{12,14},{13,15},{20,22},{21,23},{28,30},{29,31}} | collective-permute-start | bytes 1572872 | tf_op jit(solution)/shard_map/ppermute | solution.py:29
  283.8 14.9 %collective-permute-start.61 = (bf16[256,1024]{1,0:T(8,128)(2,1)S(1)}, bf16[256,1024]{1,0:T(8,128)(2,1)S(1)}, u32[]{:S(2)}, u32[]{:S(2)}) collective-permute-start(bf16[256,1024]{1,0:T(8,128)(2,1)S(1)} %get-tuple-element.200.refs_3_), channel_id=1, source_target_pairs={{0,1},{1,0},{2,3},{3,2},{4,5},{5,4},{6,7},{7,6},{8,9},{9,8},{10,11... | collective-permute-start | bytes 1572872 | tf_op jit(solution)/shard_map/ppermute | solution.py:29
  284.5 22.6 %collective-permute-start.54 = (bf16[256,1024]{1,0:T(8,128)(2,1)S(1)}, bf16[256,1024]{1,0:T(8,128)(2,1)S(1)}, u32[]{:S(2)}, u32[]{:S(2)}) collective-permute-start(bf16[256,1024]{1,0:T(8,128)(2,1)S(1)} %get-tuple-element.185.refs_3_), channel_id=1, source_target_pairs={{0,1},{1,0},{2,3},{3,2},{4,5},{5,4},{6,7},{7,6},{8,9},{9,8},{10,11... | collective-permute-start | bytes 1572872 | tf_op jit(solution)/shard_map/ppermute | solution.py:29
  (48 other events, 1014.0 us)
where the time goes:
time: 317 us; the launch traced here: 315 us
  waiting for transfers between devices  128 us (40%)
  starting transfers between devices  79.8 us (25%)
  Pallas kernels  75 us (24%)
  local copies, waits for them, and re-layouts  20.2 us (6%)
  other arithmetic  10.6 us (3%)
    ppermute x62, waiting for transfers between devices, _permute(): return lax.ppermute(value, axis, pairs)  128 us
    ppermute x62, starting transfers between devices, _permute(): return lax.ppermute(value, axis, pairs)  79.8 us
    pallas_call x4, Pallas kernels, code_terms(): pl.pallas_call(functools.partial(_code_kernel, zc, pieces, chunk * blocks...  25.1 us
    pallas_call x2, Pallas kernels, attend(): pl.pallas_call(functools.partial(_attend_kernel, heads, tile, span), grid...  18.2 us
    pallas_call x2, Pallas kernels, norm_rows(): pl.pallas_call(functools.partial(_norm_kernel, n), grid_spec=grid_spec, o...  15.1 us
    pallas_call x2, Pallas kernels, project_queries(): pl.pallas_call(functools.partial(_query_kernel, n, heads), grid_spec=grid...  14.5 us
    unnamed x100, local copies, waits for them, and re-layouts  10.2 us
  transfers between devices with their start and end apart: 62, of which 30 were waited for; matrix products, arithmetic and copies ran while one was open for 6% of the time, Pallas kernels for 19%

commit v1 on v0

--- a/solution.py
+++ b/solution.py
@@ -168,67 +168,110 @@
 
 
 def _attend_kernel(heads, tile, span, info, q_ref, k_ref, v_ref, out, s_ref, m_ref, l_ref, acc_ref):
-    step = pl.program_id(0)
     scale = LOG2E / math.sqrt(HD)
     m = heads * tile
-    q = q_ref[...].reshape(m, HD)
-    first_pos = info[0] + step * tile
-    row_pos = first_pos + lax.rem(lax.broadcasted_iota(jnp.int32, (m, CK), 0), tile)
-
-    def scores(base, j, masked):
-        keys = k_ref[pl.ds(pl.multiple_of(base + j * CK, CK), CK), :]
+    chunks = span // CK
+    tiles = q_ref.shape[1] // tile
+    blocks = k_ref.shape[0] // span
+
+    def queries(t):
+        return q_ref[:, t * tile : (t + 1) * tile, :].reshape(m, HD)
+
+    def extent(t, b):
+        if b == 0:
+            return chunks, chunks
+        first = info[0] + t * tile - b * span
+        return jnp.clip((first + 1) // CK, 0, chunks), jnp.clip((first + tile - 1) // CK + 1, 0, chunks)
+
+    def scores(q, t, b, slot, j, masked):
+        keys = k_ref[pl.ds(pl.multiple_of(b * span + j * CK, CK), CK), :]
         s = lax.dot_general(q, keys, (((1,), (1,)), ((), ())), preferred_element_type=jnp.float32)
         if masked:
-            col = base + j * CK + lax.broadcasted_iota(jnp.int32, (m, CK), 1)
-            s = jnp.where(col <= row_pos, s, -1e30)
-        s_ref[:, pl.ds(pl.multiple_of(j * CK, CK), CK)] = s
+            row = lax.rem(lax.broadcasted_iota(jnp.int32, (m, CK), 0), tile)
+            col = lax.broadcasted_iota(jnp.int32, (m, CK), 1)
+            s = jnp.where(col - row <= info[0] + t * tile - b * span - j * CK, s, -1e30)
+        s_ref[slot, :, pl.ds(pl.multiple_of(j * CK, CK), CK)] = s
         top = m_ref[...]
         for c in range(CK // 128):
             top = jnp.maximum(top, s[:, c * 128 : (c + 1) * 128])
         m_ref[...] = top
 
-    def weigh(base, j, top):
-        s = s_ref[:, pl.ds(pl.multiple_of(j * CK, CK), CK)]
+    def weigh(b, slot, j, top):
+        s = s_ref[slot, :, pl.ds(pl.multiple_of(j * CK, CK), CK)]
         p = jnp.exp2((s - top) * scale)
         total = l_ref[...]
         for c in range(CK // 128):
             total = total + p[:, c * 128 : (c + 1) * 128]
         l_ref[...] = total
-        vals = v_ref[pl.ds(pl.multiple_of(base + j * CK, CK), CK), :]
+        vals = v_ref[pl.ds(pl.multiple_of(b * span + j * CK, CK), CK), :]
         acc_ref[...] += jnp.dot(p.astype(jnp.bfloat16), vals, preferred_element_type=jnp.float32)
 
-    def block(base, full, count):
-        m_ref[...] = jnp.full(m_ref.shape, -1e30, jnp.float32)
-        l_ref[...] = jnp.zeros(l_ref.shape, jnp.float32)
-        acc_ref[...] = jnp.zeros(acc_ref.shape, jnp.float32)
-
-        def loop(n, f):
-            lax.fori_loop(0, n, lambda j, c: (f(j), c)[1], 0)
-
-        loop(full, lambda j: scores(base, j, False))
-        if count is not full:
-            lax.fori_loop(full, count, lambda j, c: (scores(base, j, True), c)[1], 0)
-        top = jnp.max(m_ref[...], axis=1, keepdims=True)
-        loop(count, lambda j: weigh(base, j, top))
-        return top, jnp.sum(l_ref[...], axis=1, keepdims=True), acc_ref[...]
-
-    chunks = span // CK
-    blocks = k_ref.shape[0] // span
-    top, total, acc = block(0, chunks, chunks)
-    for b in range(1, blocks):
-        base = b * span
-        full = jnp.clip((first_pos + 1 - base) // CK, 0, chunks)
-        count = jnp.clip((first_pos + tile - 1 - base) // CK + 1, 0, chunks)
-        top2, total2, acc2 = block(base, full, count)
-        new = jnp.maximum(top, top2)
-        f1 = jnp.exp2((top - new) * scale)
-        f2 = jnp.exp2((top2 - new) * scale)
-        acc = f1 * acc + f2 * acc2
-        total = f1 * total + f2 * total2
-        top = new
-    res = (acc / total).astype(jnp.bfloat16)
-    for h in range(heads):
-        out[:, h * HD : (h + 1) * HD] = res[h * tile : (h + 1) * tile]
+    def loop(low, high, f):
+        if not (isinstance(low, int) and isinstance(high, int) and low >= high):
+            lax.fori_loop(low, high, lambda j, c: (f(j), c)[1], 0)
+
+    def least(x, y):
+        return min(x, y) if isinstance(x, int) and isinstance(y, int) else jnp.minimum(x, y)
+
+    def most(x, y):
+        return max(x, y) if isinstance(x, int) and isinstance(y, int) else jnp.maximum(x, y)
+
+    def phase(ahead, behind):
+        full = count = seen = 0
+        if ahead:
+            t, b, slot = ahead
+            q = queries(t)
+            full, count = extent(t, b)
+            m_ref[...] = jnp.full(m_ref.shape, -1e30, jnp.float32)
+        if behind:
+            t2, b2, slot2, top = behind
+            seen = extent(t2, b2)[1]
+            l_ref[...] = jnp.zeros(l_ref.shape, jnp.float32)
+            acc_ref[...] = jnp.zeros(acc_ref.shape, jnp.float32)
+
+        def both(masked):
+            def step(j):
+                scores(q, t, b, slot, j, masked)
+                weigh(b2, slot2, j, top)
+
+            return step
+
+        x, y = least(full, seen), least(count, seen)
+        if ahead and behind:
+            loop(0, x, both(False))
+            if b > 0:
+                loop(x, y, both(True))
+        if ahead:
+            loop(x, full, lambda j: scores(q, t, b, slot, j, False))
+            if b > 0:
+                loop(most(y, full), count, lambda j: scores(q, t, b, slot, j, True))
+        if behind:
+            loop(y, seen, lambda j: weigh(b2, slot2, j, top))
+        new_top = jnp.max(m_ref[...], axis=1, keepdims=True) if ahead else None
+        return new_top, (jnp.sum(l_ref[...], axis=1, keepdims=True), acc_ref[...]) if behind else None
+
+    jobs = [(t, b) for t in range(tiles) for b in range(blocks)]
+    behind = None
+    state = None
+    for i, job in enumerate(jobs + [None]):
+        slot = i % 2
+        top, weighed = phase(job + (slot,) if job else None, behind)
+        if weighed:
+            t2, b2, _, top2 = behind
+            total2, acc2 = weighed
+            if b2 == 0:
+                state = top2, total2, acc2
+            else:
+                top1, total1, acc1 = state
+                new = jnp.maximum(top1, top2)
+                f1 = jnp.exp2((top1 - new) * scale)
+                f2 = jnp.exp2((top2 - new) * scale)
+                state = new, f1 * total1 + f2 * total2, f1 * acc1 + f2 * acc2
+            if b2 == blocks - 1:
+                res = (state[2] / state[1]).astype(jnp.bfloat16)
+                for h in range(heads):
+                    out[t2 * tile : (t2 + 1) * tile, h * HD : (h + 1) * HD] = res[h * tile : (h + 1) * tile]
+        behind = job + (slot, top) if job else None
 
 
 def attend(q, keys, values, start, span):
@@ -238,15 +281,15 @@
     total = keys.shape[0]
     grid_spec = pltpu.PrefetchScalarGridSpec(
         num_scalar_prefetch=1,
-        grid=(rows // tile,),
+        grid=(1,),
         in_specs=[
-            pl.BlockSpec((heads, tile, HD), lambda i, info: (0, i, 0)),
+            pl.BlockSpec((heads, rows, HD), lambda i, info: (0, 0, 0), pipeline_mode=pl.Buffered(1)),
             pl.BlockSpec((total, HD), lambda i, info: (0, 0), pipeline_mode=pl.Buffered(1)),
             pl.BlockSpec((total, HD), lambda i, info: (0, 0), pipeline_mode=pl.Buffered(1)),
         ],
-        out_specs=pl.BlockSpec((tile, heads * HD), lambda i, info: (i, 0)),
+        out_specs=pl.BlockSpec((rows, heads * HD), lambda i, info: (0, 0)),
         scratch_shapes=[
-            pltpu.VMEM((m, span), jnp.float32),
+            pltpu.VMEM((2, m, span), jnp.float32),
             pltpu.VMEM((m, 128), jnp.float32),
             pltpu.VMEM((m, 128), jnp.float32),
             pltpu.VMEM((m, HD), jnp.float32),

time: 317 us -> 327 us (1.032); the launches traced: 315 us -> 321 us
  Pallas kernels: 75 us -> 83.4 us
    pallas_call x2, Pallas kernels: 18.2 us -> 26.6 us  [attend(): pl.pallas_call(functools.partial(_attend_kernel, heads, tile, span), grid...]
  transfers between devices with their start and end apart: 62 -> 62, of which waited for: 30 -> 30; matrix products, arithmetic and copies ran while one was open for 6% -> 6% of each run, Pallas kernels for 19% -> 21%
where the time goes in v1:
time: 327 us; the launch traced here: 321 us
  waiting for transfers between devices  126 us (39%)
  Pallas kernels  83.4 us (26%)
  starting transfers between devices  77.8 us (24%)
  local copies, waits for them, and re-layouts  20.2 us (6%)
  other arithmetic  10.6 us (3%)
    ppermute x62, waiting for transfers between devices, _permute(): return lax.ppermute(value, axis, pairs)  126 us
    ppermute x62, starting transfers between devices, _permute(): return lax.ppermute(value, axis, pairs)  77.8 us
    pallas_call x2, Pallas kernels, attend(): pl.pallas_call(functools.partial(_attend_kernel, heads, tile, span), grid...  26.6 us
    pallas_call x4, Pallas kernels, code_terms(): pl.pallas_call(functools.partial(_code_kernel, zc, pieces, chunk * blocks...  25.1 us
    pallas_call x2, Pallas kernels, norm_rows(): pl.pallas_call(functools.partial(_norm_kernel, n), grid_spec=grid_spec, o...  15.1 us
    pallas_call x2, Pallas kernels, project_queries(): pl.pallas_call(functools.partial(_query_kernel, n, heads), grid_spec=grid...  14.5 us
    unnamed x100, local copies, waits for them, and re-layouts  10.2 us
  transfers between devices with their start and end apart: 62, of which 30 were waited for; matrix products, arithmetic and copies ran while one was open for 6% of the time, Pallas kernels for 21%

profile of v1, /device:TPU:0, one launch (start us, length us, event | category | flops | bytes accessed | tf_op | source)
XLA Modules:
  0.0 320.6 jit_solution(15512660070135810749)
XLA Ops:
  1.3 3.0 collective-permute-start.2
  4.3 4.3 %collective-permute-start.1 = (bf16[256,1024]{1,0:T(8,128)(2,1)S(1)}, bf16[256,1024]{1,0:T(8,128)(2,1)}, u32[]{:S(2)}, u32[]{:S(2)}) collective-permute-start(bf16[256,1024]{1,0:T(8,128)(2,1)S(1)} %get-tuple-element.208.refs_0_), channel_id=1, source_target_pairs={{0,2},{1,3},{2,4},{3,5},{4,6},{5,7},{8,10},{9,11},{10,12},{11,13},... | collective-permute-start | bytes 1572872 | tf_op jit(solution)/shard_map/ppermute | solution.py:29
  9.9 2.3 constant_dynamic-slice_fusion
  12.9 2.3 constant_dynamic-slice_fusion.1
  16.3 2.4 collective-permute-done.1
  18.7 4.9 %collective-permute-done = bf16[256,1024]{1,0:T(8,128)(2,1)S(1)} collective-permute-done((bf16[256,1024]{1,0:T(8,128)(2,1)S(1)}, bf16[256,1024]{1,0:T(8,128)(2,1)S(1)}, u32[]{:S(2)}, u32[]{:S(2)}) %collective-permute-start) | collective-permute-done | bytes 524320 | tf_op jit(solution)/shard_map/ppermute | solution.py:29
  26.3 1.8 multiply_sine_fusion
  30.6 1.6 collective-permute-start.5
  32.2 8.7 %collective-permute-start.4 = (bf16[256,1024]{1,0:T(8,128)(2,1)S(1)}, bf16[256,1024]{1,0:T(8,128)(2,1)S(1)}, u32[]{:S(2)}, u32[]{:S(2)}) collective-permute-start(bf16[256,1024]{1,0:T(8,128)(2,1)S(1)} %get-tuple-element.137.refs_0_), channel_id=1, source_target_pairs={{0,2},{1,3},{2,4},{3,5},{4,6},{5,7},{8,10},{9,11},{10,12},{11,13},... | collective-permute-start | bytes 1572872 | tf_op jit(solution)/shard_map/ppermute | solution.py:29
  42.5 3.3 %fusion.3 = (bf16[128,2048]{1,0:T(8,128)(2,1)}, bf16[128,2048]{1,0:T(8,128)(2,1)}, bf16[128,2048]{1,0:T(8,128)(2,1)S(1)}) fusion(bf16[512,8192]{1,0:T(8,128)(2,1)} %refs_4_.7, s32[]{:T(128)S(6)} %dynamic_slice.22, s32[]{:T(128)S(6)} %select_n.270, s32[]{:T(128)S(6)} %select_n.267, s32[]{:T(128)S(6)} %select_n.251), kind=kLoop, calls=%fused_computation.33 | loop fusion | bytes 3145744 | tf_op jit(solution)/shard_map/dynamic_slice | solution.py:551
  47.2 2.0 collective-permute-done.5.refs_4_
  51.2 3.9 %collective-permute-done.3 = bf16[256,1024]{1,0:T(8,128)(2,1)S(1)} collective-permute-done((bf16[256,1024]{1,0:T(8,128)(2,1)S(1)}, bf16[256,1024]{1,0:T(8,128)(2,1)S(1)}, u32[]{:S(2)}, u32[]{:S(2)}) %collective-permute-start.3) | collective-permute-done | bytes 524320 | tf_op jit(solution)/shard_map/ppermute | solution.py:29
  56.4 2.0 select_bitcast_fusion.1
  58.4 1.6 collective-permute-start.8
  60.0 5.7 %collective-permute-done.15 = bf16[256,1024]{1,0:T(8,128)(2,1)S(1)} collective-permute-done((bf16[256,1024]{1,0:T(8,128)(2,1)}, bf16[256,1024]{1,0:T(8,128)(2,1)S(1)}, u32[]{:S(2)}, u32[]{:S(2)}) %collective-permute-start.15) | collective-permute-done | bytes 524320 | tf_op jit(solution)/shard_map/ppermute | solution.py:29
  66.9 1.6 select_bitcast_fusion.3
  68.6 1.4 collective-permute-done.17.refs_6_
  70.0 6.0 %collective-permute-done.8.refs_5_ = bf16[256,1024]{1,0:T(8,128)(2,1)S(1)} collective-permute-done((bf16[256,1024]{1,0:T(8,128)(2,1)S(1)}, bf16[256,1024]{1,0:T(8,128)(2,1)S(1)}, u32[]{:S(2)}, u32[]{:S(2)}) %collective-permute-start.8) | collective-permute-done | bytes 524320 | tf_op jit(solution)/shard_map/ppermute | solution.py:29
  76.0 2.7 collective-permute-done.6
  81.4 2.8 collective-permute-start.18
  84.3 1.6 collective-permute-start.20
  86.0 7.7 %collective-permute-done.11.refs_6_ = bf16[256,1024]{1,0:T(8,128)(2,1)S(1)} collective-permute-done((bf16[256,1024]{1,0:T(8,128)(2,1)S(1)}, bf16[256,1024]{1,0:T(8,128)(2,1)S(1)}, u32[]{:S(2)}, u32[]{:S(2)}) %collective-permute-start.11) | collective-permute-done | bytes 524320 | tf_op jit(solution)/shard_map/ppermute | solution.py:29
  93.7 9.8 %collective-permute-done.18.refs_9_ = bf16[128,2048]{1,0:T(8,128)(2,1)S(1)} collective-permute-done((bf16[128,2048]{1,0:T(8,128)(2,1)S(1)}, bf16[128,2048]{1,0:T(8,128)(2,1)S(1)}, u32[]{:S(2)}, u32[]{:S(2)}) %collective-permute-start.18) | collective-permute-done | bytes 524320 | tf_op jit(solution)/shard_map/ppermute | solution.py:29
  103.5 2.1 collective-permute-start.36
  105.8 7.3 %query_projection.2.q_ref = bf16[4,256,128]{2,1,0:T(8,128)(2,1)S(1)} custom-call(s32[8]{0:T(128)S(1)} %stack.110.ids, bf16[256,1024]{1,0:T(8,128)(2,1)S(1)} %copy-done.16, bf16[256,1024]{1,0:T(8,128)(2,1)S(1)} %copy-done.12, bf16[256,1024]{1,0:T(8,128)(2,1)S(1)} %select_select_fusion.5.refs_2_, bf16[256,1024]{1,0:T(8,128)(2,1)S(1)} %select_select_fusion.4.refs_3_, ...), custom_call_target="tpu_custom_call" | custom-call | flops 107374184 | bytes 629145 | tf_op jit(solution)/shard_map/query_projection/pallas_call | solution.py:157
  113.1 1.6 collective-permute-start.19
  114.7 1.5 collective-permute-start.33
  116.4 13.4 %attend.2.refs_0_ = bf16[256,512]{1,0:T(8,128)(2,1)S(1)} custom-call(s32[1]{0:T(128)} %bitcast.17.info, bf16[4,256,128]{2,1,0:T(8,128)(2,1)S(1)} %query_projection.2.q_ref, bf16[8192,128]{1,0:T(8,128)(2,1)S(1)} %bitcast.36, bf16[8192,128]{1,0:T(8,128)(2,1)S(1)} %bitcast.34), custom_call_target="tpu_custom_call" | custom-call | flops 214748368 | bytes 209715 | tf_op jit(solution)/shard_map/attend/pallas_call | solution.py:298
  131.2 7.3 %query_projection.3.q_ref = bf16[4,256,128]{2,1,0:T(8,128)(2,1)S(1)} custom-call(s32[8]{0:T(128)S(1)} %stack.110.ids, bf16[256,1024]{1,0:T(8,128)(2,1)S(1)} %copy-done.14, bf16[256,1024]{1,0:T(8,128)(2,1)S(1)} %broadcast_select_fusion.3.refs_1_, bf16[256,1024]{1,0:T(8,128)(2,1)S(1)} %select_select_fusion.7.refs_2_, ...), custom_call_target="tpu_custom_call" | custom-call | flops 107374184 | bytes 629145 | tf_op jit(solution)/shard_map/query_projection/pallas_call | solution.py:157
  139.2 2.0 collective-permute-start.30
  141.2 3.8 %collective-permute-start.28 = (bf16[256,512]{1,0:T(8,128)(2,1)S(1)}, bf16[256,512]{1,0:T(8,128)(2,1)}, u32[]{:S(2)}, u32[]{:S(2)}) collective-permute-start(bf16[256,512]{1,0:T(8,128)(2,1)S(1)} %attend.2.refs_0_), channel_id=1, source_target_pairs={{0,6},{1,7},{2,0},{3,1},{4,2},{5,3},{6,4},{7,5},{8,14},{9,15},{10,... | collective-permute-start | bytes 786440 | tf_op jit(solution)/shard_map/ppermute | solution.py:29
  146.1 1.6 copy-done.1
  148.6 13.2 %attend.3.refs_0_ = bf16[256,512]{1,0:T(8,128)(2,1)S(1)} custom-call(s32[1]{0:T(128)} %bitcast.16.info, bf16[4,256,128]{2,1,0:T(8,128)(2,1)S(1)} %copy-done.22, bf16[8192,128]{1,0:T(8,128)(2,1)S(1)} %bitcast.37, bf16[8192,128]{1,0:T(8,128)(2,1)S(1)} %bitcast.35), custom_call_target="tpu_custom_call" | custom-call | flops 214748368 | bytes 209715 | tf_op jit(solution)/shard_map/attend/pallas_call | solution.py:298
  163.0 3.2 %collective-permute-done.27.refs_2_ = bf16[256,512]{1,0:T(8,128)(2,1)} collective-permute-done((bf16[256,512]{1,0:T(8,128)(2,1)S(1)}, bf16[256,512]{1,0:T(8,128)(2,1)}, u32[]{:S(2)}, u32[]{:S(2)}) %collective-permute-start.27) | collective-permute-done | bytes 262176 | tf_op jit(solution)/shard_map/ppermute | solution.py:29
  167.0 2.2 collective-permute-done.39.refs_16_
  170.7 6.4 %code_terms.5 = bf16[256,1024]{1,0:T(8,128)(2,1)} custom-call(s32[6]{0:T(128)S(1)} %stack.126.info, bf16[256,512]{1,0:T(8,128)(2,1)S(1)} %attend.2.refs_0_, bf16[256,512]{1,0:T(8,128)(2,1)} %collective-permute-done.26.refs_1_, bf16[256,512]{1,0:T(8,128)(2,1)} %collective-permute-done.27.refs_2_, bf16[256,512]{1,0:T(8,128)(2,1)} %collective-permute-done.28.refs_3_, ...), custom_call_target="tpu_custom_call" | custom-call | flops 107374184 | bytes 209715 | tf_op jit(solution)/shard_map/code_terms/pallas_call | solution.py:387
  177.6 1.5 collective-permute-start.25
  179.2 2.1 collective-permute-start.24
  181.3 2.0 collective-permute-start.23
  183.4 6.4 %code_terms.4.mine = f32[256,1024]{1,0:T(8,128)} custom-call(s32[6]{0:T(128)S(1)} %stack.117.info, bf16[256,512]{1,0:T(8,128)(2,1)S(1)} %attend.2.refs_0_, bf16[256,512]{1,0:T(8,128)(2,1)} %collective-permute-done.26.refs_1_, bf16[256,512]{1,0:T(8,128)(2,1)} %collective-permute-done.27.refs_2_, bf16[256,512]{1,0:T(8,128)(2,1)} %collective-permute-done.28.refs_3_, ...), custom_call_target="tpu_custom_call" | custom-call | flops 107374184 | bytes 209715 | tf_op jit(solution)/shard_map/code_terms/pallas_call | solution.py:387
  189.8 1.5 collective-permute-done.40.theirs
  192.6 1.6 residual.2.refs_0_
  194.8 3.6 %collective-permute-start.43 = (bf16[256,1024]{1,0:T(8,128)(2,1)S(1)}, bf16[256,1024]{1,0:T(8,128)(2,1)S(1)}, u32[]{:S(2)}, u32[]{:S(2)}) collective-permute-start(bf16[256,1024]{1,0:T(8,128)(2,1)S(1)} %residual.2.refs_0_), channel_id=1, source_target_pairs={{0,2},{1,3},{2,4},{3,5},{4,6},{5,7},{8,10},{9,11},{10,12},{11,13},... | collective-permute-start | bytes 1572872 | tf_op jit(solution)/shard_map/ppermute | solution.py:29
  198.4 1.5 collective-permute-start.42
  199.9 5.3 %collective-permute-done.24.refs_2_ = bf16[256,512]{1,0:T(8,128)(2,1)} collective-permute-done((bf16[256,512]{1,0:T(8,128)(2,1)S(1)}, bf16[256,512]{1,0:T(8,128)(2,1)}, u32[]{:S(2)}, u32[]{:S(2)}) %collective-permute-start.24) | collective-permute-done | bytes 262176 | tf_op jit(solution)/shard_map/ppermute | solution.py:29
  205.2 5.9 %code_terms.6 = bf16[256,1024]{1,0:T(8,128)(2,1)S(1)} custom-call(s32[6]{0:T(128)S(1)} %stack.126.info, bf16[256,512]{1,0:T(8,128)(2,1)S(1)} %copy-done.10, bf16[256,512]{1,0:T(8,128)(2,1)} %collective-permute-done.23.refs_1_, bf16[256,512]{1,0:T(8,128)(2,1)} %collective-permute-done.24.refs_2_, bf16[256,512]{1,0:T(8,128)(2,1)} %collective-permute-done.25.refs_3_, ...), custom_call_target="tpu_custom_call" | custom-call | flops 107374184 | bytes 209715 | tf_op jit(solution)/shard_map/code_terms/pallas_call | solution.py:387
  211.1 1.7 collective-permute-start.41
  212.8 6.4 %code_terms.7.mine = f32[256,1024]{1,0:T(8,128)} custom-call(s32[6]{0:T(128)S(1)} %stack.117.info, bf16[256,512]{1,0:T(8,128)(2,1)S(1)} %copy-done.10, bf16[256,512]{1,0:T(8,128)(2,1)} %collective-permute-done.23.refs_1_, bf16[256,512]{1,0:T(8,128)(2,1)} %collective-permute-done.24.refs_2_, bf16[256,512]{1,0:T(8,128)(2,1)} %collective-permute-done.25.refs_3_, ...), custom_call_target="tpu_custom_call" | custom-call | flops 107374184 | bytes 209715 | tf_op jit(solution)/shard_map/code_terms/pallas_call | solution.py:387
  219.3 4.3 %collective-permute-done.41.theirs = bf16[256,1024]{1,0:T(8,128)(2,1)S(1)} collective-permute-done((bf16[256,1024]{1,0:T(8,128)(2,1)S(1)}, bf16[256,1024]{1,0:T(8,128)(2,1)S(1)}, u32[]{:S(2)}, u32[]{:S(2)}) %collective-permute-start.41) | collective-permute-done | bytes 524320 | tf_op jit(solution)/shard_map/ppermute | solution.py:29
  225.4 1.6 collective-permute-start.47
  230.9 9.4 %collective-permute-done.47.refs_4_ = bf16[256,1024]{1,0:T(8,128)(2,1)S(1)} collective-permute-done((bf16[256,1024]{1,0:T(8,128)(2,1)S(1)}, bf16[256,1024]{1,0:T(8,128)(2,1)S(1)}, u32[]{:S(2)}, u32[]{:S(2)}) %collective-permute-start.47) | collective-permute-done | bytes 524320 | tf_op jit(solution)/shard_map/ppermute | solution.py:29
  241.6 3.9 %collective-permute-done.45 = bf16[256,1024]{1,0:T(8,128)(2,1)S(1)} collective-permute-done((bf16[256,1024]{1,0:T(8,128)(2,1)S(1)}, bf16[256,1024]{1,0:T(8,128)(2,1)S(1)}, u32[]{:S(2)}, u32[]{:S(2)}) %collective-permute-start.45) | collective-permute-done | bytes 524320 | tf_op jit(solution)/shard_map/ppermute | solution.py:29
  248.1 3.4 %collective-permute-done.57.refs_5_ = bf16[256,1024]{1,0:T(8,128)(2,1)S(1)} collective-permute-done((bf16[256,1024]{1,0:T(8,128)(2,1)S(1)}, bf16[256,1024]{1,0:T(8,128)(2,1)S(1)}, u32[]{:S(2)}, u32[]{:S(2)}) %collective-permute-start.57) | collective-permute-done | bytes 524320 | tf_op jit(solution)/shard_map/ppermute | solution.py:29
  251.5 4.6 %collective-permute-done.55 = bf16[256,1024]{1,0:T(8,128)(2,1)S(1)} collective-permute-done((bf16[256,1024]{1,0:T(8,128)(2,1)S(1)}, bf16[256,1024]{1,0:T(8,128)(2,1)S(1)}, u32[]{:S(2)}, u32[]{:S(2)}) %collective-permute-start.55) | collective-permute-done | bytes 524320 | tf_op jit(solution)/shard_map/ppermute | solution.py:29
  258.9 3.9 %collective-permute-done.50.refs_5_ = bf16[256,1024]{1,0:T(8,128)(2,1)S(1)} collective-permute-done((bf16[256,1024]{1,0:T(8,128)(2,1)S(1)}, bf16[256,1024]{1,0:T(8,128)(2,1)S(1)}, u32[]{:S(2)}, u32[]{:S(2)}) %collective-permute-start.50) | collective-permute-done | bytes 524320 | tf_op jit(solution)/shard_map/ppermute | solution.py:29
  262.8 6.3 %collective-permute-done.48 = bf16[256,1024]{1,0:T(8,128)(2,1)S(1)} collective-permute-done((bf16[256,1024]{1,0:T(8,128)(2,1)S(1)}, bf16[256,1024]{1,0:T(8,128)(2,1)S(1)}, u32[]{:S(2)}, u32[]{:S(2)}) %collective-permute-start.48) | collective-permute-done | bytes 524320 | tf_op jit(solution)/shard_map/ppermute | solution.py:29
  271.0 3.0 collective-permute-done.60.refs_6_
  274.7 5.6 %collective-permute-done.58 = bf16[256,1024]{1,0:T(8,128)(2,1)S(1)} collective-permute-done((bf16[256,1024]{1,0:T(8,128)(2,1)S(1)}, bf16[256,1024]{1,0:T(8,128)(2,1)S(1)}, u32[]{:S(2)}, u32[]{:S(2)}) %collective-permute-start.58) | collective-permute-done | bytes 524320 | tf_op jit(solution)/shard_map/ppermute | solution.py:29
  280.3 1.6 collective-permute-done.53.refs_6_
  281.9 6.3 %collective-permute-done.51 = bf16[256,1024]{1,0:T(8,128)(2,1)S(1)} collective-permute-done((bf16[256,1024]{1,0:T(8,128)(2,1)S(1)}, bf16[256,1024]{1,0:T(8,128)(2,1)S(1)}, u32[]{:S(2)}, u32[]{:S(2)}) %collective-permute-start.51) | collective-permute-done | bytes 524320 | tf_op jit(solution)/shard_map/ppermute | solution.py:29
  289.0 1.5 collective-permute-start.54
  291.2 12.2 %collective-permute-done.61.refs_7_ = bf16[256,1024]{1,0:T(8,128)(2,1)S(1)} collective-permute-done((bf16[256,1024]{1,0:T(8,128)(2,1)S(1)}, bf16[256,1024]{1,0:T(8,128)(2,1)S(1)}, u32[]{:S(2)}, u32[]{:S(2)}) %collective-permute-start.61) | collective-permute-done | bytes 524320 | tf_op jit(solution)/shard_map/ppermute | solution.py:29
  304.2 7.5 %norm.2.refs_10_ = bf16[512,8192]{1,0:T(8,128)(2,1)} custom-call(s32[8]{0:T(128)} %copy-done.30, bf16[256,1024]{1,0:T(8,128)(2,1)} %copy-done.17, bf16[256,1024]{1,0:T(8,128)(2,1)} %copy-done.34, bf16[256,1024]{1,0:T(8,128)(2,1)} %copy-done.36, bf16[256,1024]{1,0:T(8,128)(2,1)} %copy-done.33, bf16[256,1024]{1,0:T(8,128)(2,1)} %copy-done.39, ...), custom_call_target="tpu_custom_call" | custom-call | flops 838860 | bytes 419430 | tf_op jit(solution)/shard_map/norm/pallas_call | solution.py:474
  312.6 7.5 %norm.3 = bf16[512,8192]{1,0:T(8,128)(2,1)} custom-call(s32[8]{0:T(128)} %copy-done.30, bf16[256,1024]{1,0:T(8,128)(2,1)} %copy-done.18, bf16[256,1024]{1,0:T(8,128)(2,1)} %copy-done.35, bf16[256,1024]{1,0:T(8,128)(2,1)} %copy-done.37, bf16[256,1024]{1,0:T(8,128)(2,1)} %copy-done.32, bf16[256,1024]{1,0:T(8,128)(2,1)} %copy-done.40, ...), custom_call_target="tpu_custom_call", output_to_operand_aliasing={{}: (11, {})} | custom-call | flops 838860 | bytes 419430 | tf_op jit(solution)/shard_map/norm/pallas_call | solution.py:474
  (201 shorter events, 47.5 us)
Async XLA Ops:
  1.3 15.0 %collective-permute-start.2 = (bf16[256,1024]{1,0:T(8,128)(2,1)S(1)}, bf16[256,1024]{1,0:T(8,128)(2,1)S(1)}, u32[]{:S(2)}, u32[]{:S(2)}) collective-permute-start(bf16[256,1024]{1,0:T(8,128)(2,1)S(1)} %get-tuple-element.208.refs_0_), channel_id=1, source_target_pairs={{0,1},{1,0},{2,3},{3,2},{4,5},{5,4},{6,7},{7,6},{8,9},{9,8},{10,11... | collective-permute-start | bytes 1572872 | tf_op jit(solution)/shard_map/ppermute | solution.py:29
  4.3 14.4 %collective-permute-start.1 = (bf16[256,1024]{1,0:T(8,128)(2,1)S(1)}, bf16[256,1024]{1,0:T(8,128)(2,1)}, u32[]{:S(2)}, u32[]{:S(2)}) collective-permute-start(bf16[256,1024]{1,0:T(8,128)(2,1)S(1)} %get-tuple-element.208.refs_0_), channel_id=1, source_target_pairs={{0,2},{1,3},{2,4},{3,5},{4,6},{5,7},{8,10},{9,11},{10,12},{11,13},... | collective-permute-start | bytes 1572872 | tf_op jit(solution)/shard_map/ppermute | solution.py:29
  8.6 15.0 %collective-permute-start = (bf16[256,1024]{1,0:T(8,128)(2,1)S(1)}, bf16[256,1024]{1,0:T(8,128)(2,1)S(1)}, u32[]{:S(2)}, u32[]{:S(2)}) collective-permute-start(bf16[256,1024]{1,0:T(8,128)(2,1)S(1)} %get-tuple-element.208.refs_0_), channel_id=1, source_target_pairs={{2,0},{3,1},{4,2},{5,3},{6,4},{7,5},{10,8},{11,9},{12,10},{13,11},... | collective-permute-start | bytes 1572872 | tf_op jit(solution)/shard_map/ppermute | solution.py:29
  12.2 43.5 %collective-permute-start.22 = (bf16[4096,128]{1,0:T(8,128)(2,1)}, bf16[4096,128]{1,0:T(8,128)(2,1)}, u32[]{:S(2)}, u32[]{:S(2)}) collective-permute-start(bf16[4096,128]{1,0:T(8,128)(2,1)} %constant_dynamic-slice_fusion), channel_id=1, source_target_pairs={{0,8},{8,0},{1,9},{9,1},{2,10},{10,2},{3,11},{11,3},{4,12},{12,4},... | collective-permute-start | bytes 3145736 | tf_op jit(solution)/shard_map/ppermute | solution.py:29
  23.7 8.5 %collective-permute-start.13 = (bf16[256,1024]{1,0:T(8,128)(2,1)}, bf16[256,1024]{1,0:T(8,128)(2,1)S(1)}, u32[]{:S(2)}, u32[]{:S(2)}) collective-permute-start(bf16[256,1024]{1,0:T(8,128)(2,1)} %collective-permute-done.1), channel_id=1, source_target_pairs={{2,4},{3,5},{4,6},{5,7},{10,12},{11,13},{12,14},{13,15},{18,20},{1... | collective-permute-start | bytes 1572872 | tf_op jit(solution)/shard_map/ppermute | solution.py:29
  24.4 16.8 %collective-permute-start.12 = (bf16[256,1024]{1,0:T(8,128)(2,1)S(1)}, bf16[256,1024]{1,0:T(8,128)(2,1)}, u32[]{:S(2)}, u32[]{:S(2)}) collective-permute-start(bf16[256,1024]{1,0:T(8,128)(2,1)S(1)} %collective-permute-done), channel_id=1, source_target_pairs={{2,0},{3,1},{4,2},{5,3},{10,8},{11,9},{12,10},{13,11},{18,16},{19,... | collective-permute-start | bytes 1572872 | tf_op jit(solution)/shard_map/ppermute | solution.py:29
  25.7 20.1 %collective-permute-start.14 = (bf16[256,1024]{1,0:T(8,128)(2,1)S(1)}, bf16[256,1024]{1,0:T(8,128)(2,1)S(1)}, u32[]{:S(2)}, u32[]{:S(2)}) collective-permute-start(bf16[256,1024]{1,0:T(8,128)(2,1)S(1)} %broadcast_select_fusion.2.refs_1_), channel_id=1, source_target_pairs={{0,1},{1,0},{2,3},{3,2},{4,5},{5,4},{6,7},{7,6},{8,9},{9,8},{10,11... | collective-permute-start | bytes 1572872 | tf_op jit(solution)/shard_map/ppermute | solution.py:29
  28.1 77.7 %copy-start.28 = (f32[8192]{0:T(1024)}, f32[8192]{0:T(1024)S(1)}, u32[]{:S(2)}) copy-start(f32[8192]{0:T(1024)S(1)} %reshape.54) | copy-start | bytes 98308
  28.2 103.0 %copy-start.30 = (s32[8]{0:T(128)}, s32[8]{0:T(128)S(1)}, u32[]{:S(2)}) copy-start(s32[8]{0:T(128)S(1)} %stack.110.ids) | copy-start | bytes 100
  30.6 18.5 %collective-permute-start.5 = (bf16[256,1024]{1,0:T(8,128)(2,1)S(1)}, bf16[256,1024]{1,0:T(8,128)(2,1)S(1)}, u32[]{:S(2)}, u32[]{:S(2)}) collective-permute-start(bf16[256,1024]{1,0:T(8,128)(2,1)S(1)} %get-tuple-element.137.refs_0_), channel_id=1, source_target_pairs={{0,1},{1,0},{2,3},{3,2},{4,5},{5,4},{6,7},{7,6},{8,9},{9,8},{10,11... | collective-permute-start | bytes 1572872 | tf_op jit(solution)/shard_map/ppermute | solution.py:29
  32.2 18.3 %collective-permute-start.4 = (bf16[256,1024]{1,0:T(8,128)(2,1)S(1)}, bf16[256,1024]{1,0:T(8,128)(2,1)S(1)}, u32[]{:S(2)}, u32[]{:S(2)}) collective-permute-start(bf16[256,1024]{1,0:T(8,128)(2,1)S(1)} %get-tuple-element.137.refs_0_), channel_id=1, source_target_pairs={{0,2},{1,3},{2,4},{3,5},{4,6},{5,7},{8,10},{9,11},{10,12},{11,13},... | collective-permute-start | bytes 1572872 | tf_op jit(solution)/shard_map/ppermute | solution.py:29
  41.2 13.9 %collective-permute-start.3 = (bf16[256,1024]{1,0:T(8,128)(2,1)S(1)}, bf16[256,1024]{1,0:T(8,128)(2,1)S(1)}, u32[]{:S(2)}, u32[]{:S(2)}) collective-permute-start(bf16[256,1024]{1,0:T(8,128)(2,1)S(1)} %get-tuple-element.137.refs_0_), channel_id=1, source_target_pairs={{2,0},{3,1},{4,2},{5,3},{6,4},{7,5},{10,8},{11,9},{12,10},{13,11},... | collective-permute-start | bytes 1572872 | tf_op jit(solution)/shard_map/ppermute | solution.py:29
  45.8 12.5 %collective-permute-start.21 = (bf16[4096,128]{1,0:T(8,128)(2,1)S(1)}, bf16[4096,128]{1,0:T(8,128)(2,1)S(1)}, u32[]{:S(2)}, u32[]{:S(2)}) collective-permute-start(bf16[4096,128]{1,0:T(8,128)(2,1)S(1)} %copy-done.38), channel_id=1, source_target_pairs={{0,8},{8,0},{1,9},{9,1},{2,10},{10,2},{3,11},{11,3},{4,12},{12,4},... | collective-permute-start | bytes 3145736 | tf_op jit(solution)/shard_map/ppermute | solution.py:29
  49.2 16.5 %collective-permute-start.15 = (bf16[256,1024]{1,0:T(8,128)(2,1)}, bf16[256,1024]{1,0:T(8,128)(2,1)S(1)}, u32[]{:S(2)}, u32[]{:S(2)}) collective-permute-start(bf16[256,1024]{1,0:T(8,128)(2,1)} %collective-permute-done.12), channel_id=1, source_target_pairs={{2,0},{3,1},{10,8},{11,9},{18,16},{19,17},{26,24},{27,25}} | collective-permute-start | bytes 1572872 | tf_op jit(solution)/shard_map/ppermute | solution.py:29
  50.5 18.1 %collective-permute-start.16 = (bf16[256,1024]{1,0:T(8,128)(2,1)S(1)}, bf16[256,1024]{1,0:T(8,128)(2,1)S(1)}, u32[]{:S(2)}, u32[]{:S(2)}) collective-permute-start(bf16[256,1024]{1,0:T(8,128)(2,1)S(1)} %collective-permute-done.13), channel_id=1, source_target_pairs={{4,6},{5,7},{12,14},{13,15},{20,22},{21,23},{28,30},{29,31}} | collective-permute-start | bytes 1572872 | tf_op jit(solution)/shard_map/ppermute | solution.py:29
  55.1 14.9 %collective-permute-start.17 = (bf16[256,1024]{1,0:T(8,128)(2,1)S(1)}, bf16[256,1024]{1,0:T(8,128)(2,1)S(1)}, u32[]{:S(2)}, u32[]{:S(2)}) collective-permute-start(bf16[256,1024]{1,0:T(8,128)(2,1)S(1)} %select_select_fusion.5.refs_2_), channel_id=1, source_target_pairs={{0,1},{1,0},{2,3},{3,2},{4,5},{5,4},{6,7},{7,6},{8,9},{9,8},{10,11... | collective-permute-start | bytes 1572872 | tf_op jit(solution)/shard_map/ppermute | solution.py:29
  55.7 14.3 %collective-permute-start.7 = (bf16[256,1024]{1,0:T(8,128)(2,1)S(1)}, bf16[256,1024]{1,0:T(8,128)(2,1)S(1)}, u32[]{:S(2)}, u32[]{:S(2)}) collective-permute-start(bf16[256,1024]{1,0:T(8,128)(2,1)S(1)} %collective-permute-done.4), channel_id=1, source_target_pairs={{2,4},{3,5},{4,6},{5,7},{10,12},{11,13},{12,14},{13,15},{18,20},{1... | collective-permute-start | bytes 1572872 | tf_op jit(solution)/shard_map/ppermute | solution.py:29
  58.4 17.6 %collective-permute-start.8 = (bf16[256,1024]{1,0:T(8,128)(2,1)S(1)}, bf16[256,1024]{1,0:T(8,128)(2,1)S(1)}, u32[]{:S(2)}, u32[]{:S(2)}) collective-permute-start(bf16[256,1024]{1,0:T(8,128)(2,1)S(1)} %broadcast_select_fusion.3.refs_1_), channel_id=1, source_target_pairs={{0,1},{1,0},{2,3},{3,2},{4,5},{5,4},{6,7},{7,6},{8,9},{9,8},{10,11... | collective-permute-start | bytes 1572872 | tf_op jit(solution)/shard_map/ppermute | solution.py:29
  65.7 13.0 %collective-permute-start.6 = (bf16[256,1024]{1,0:T(8,128)(2,1)S(1)}, bf16[256,1024]{1,0:T(8,128)(2,1)S(1)}, u32[]{:S(2)}, u32[]{:S(2)}) collective-permute-start(bf16[256,1024]{1,0:T(8,128)(2,1)S(1)} %collective-permute-done.3), channel_id=1, source_target_pairs={{2,0},{3,1},{4,2},{5,3},{10,8},{11,9},{12,10},{13,11},{18,16},{19,... | collective-permute-start | bytes 1572872 | tf_op jit(solution)/shard_map/ppermute | solution.py:29
  78.8 14.9 %collective-permute-start.11 = (bf16[256,1024]{1,0:T(8,128)(2,1)S(1)}, bf16[256,1024]{1,0:T(8,128)(2,1)S(1)}, u32[]{:S(2)}, u32[]{:S(2)}) collective-permute-start(bf16[256,1024]{1,0:T(8,128)(2,1)S(1)} %select_select_fusion.7.refs_2_), channel_id=1, source_target_pairs={{0,1},{1,0},{2,3},{3,2},{4,5},{5,4},{6,7},{7,6},{8,9},{9,8},{10,11... | collective-permute-start | bytes 1572872 | tf_op jit(solution)/shard_map/ppermute | solution.py:29
  79.3 14.4 %collective-permute-start.9 = (bf16[256,1024]{1,0:T(8,128)(2,1)S(1)}, bf16[256,1024]{1,0:T(8,128)(2,1)S(1)}, u32[]{:S(2)}, u32[]{:S(2)}) collective-permute-start(bf16[256,1024]{1,0:T(8,128)(2,1)S(1)} %collective-permute-done.6), channel_id=1, source_target_pairs={{2,0},{3,1},{10,8},{11,9},{18,16},{19,17},{26,24},{27,25}} | collective-permute-start | bytes 1572872 | tf_op jit(solution)/shard_map/ppermute | solution.py:29
  80.6 13.1 %collective-permute-start.10 = (bf16[256,1024]{1,0:T(8,128)(2,1)S(1)}, bf16[256,1024]{1,0:T(8,128)(2,1)S(1)}, u32[]{:S(2)}, u32[]{:S(2)}) collective-permute-start(bf16[256,1024]{1,0:T(8,128)(2,1)S(1)} %collective-permute-done.7), channel_id=1, source_target_pairs={{4,6},{5,7},{12,14},{13,15},{20,22},{21,23},{28,30},{29,31}} | collective-permute-start | bytes 1572872 | tf_op jit(solution)/shard_map/ppermute | solution.py:29
  81.4 22.2 %collective-permute-start.18 = (bf16[128,2048]{1,0:T(8,128)(2,1)S(1)}, bf16[128,2048]{1,0:T(8,128)(2,1)S(1)}, u32[]{:S(2)}, u32[]{:S(2)}) collective-permute-start(bf16[128,2048]{1,0:T(8,128)(2,1)S(1)} %get-tuple-element.132), channel_id=1, source_target_pairs={{0,4},{1,5},{2,6},{3,7},{4,0},{5,1},{6,2},{7,3},{8,12},{9,13},{10,... | collective-permute-start | bytes 1572872 | tf_op jit(solution)/shard_map/ppermute | solution.py:29
  84.3 21.5 %collective-permute-start.20 = (bf16[256,1024]{1,0:T(8,128)(2,1)S(1)}, bf16[256,1024]{1,0:T(8,128)(2,1)S(1)}, u32[]{:S(2)}, u32[]{:S(2)}) collective-permute-start(bf16[256,1024]{1,0:T(8,128)(2,1)S(1)} %select_select_fusion.4.refs_3_), channel_id=1, source_target_pairs={{0,1},{1,0},{2,3},{3,2},{4,5},{5,4},{6,7},{7,6},{8,9},{9,8},{10,11... | collective-permute-start | bytes 1572872 | tf_op jit(solution)/shard_map/ppermute | solution.py:29
  103.5 27.6 %collective-permute-start.36 = (bf16[128,2048]{1,0:T(8,128)(2,1)}, bf16[128,2048]{1,0:T(8,128)(2,1)S(1)}, u32[]{:S(2)}, u32[]{:S(2)}) collective-permute-start(bf16[128,2048]{1,0:T(8,128)(2,1)} %get-tuple-element.156), channel_id=1, source_target_pairs={{0,6},{1,7},{2,0},{3,1},{4,2},{5,3},{6,4},{7,5},{8,14},{9,15},{10,... | collective-permute-start | bytes 1572872 | tf_op jit(solution)/shard_map/ppermute | solution.py:29
  113.1 18.0 %collective-permute-start.19 = (bf16[256,1024]{1,0:T(8,128)(2,1)S(1)}, bf16[256,1024]{1,0:T(8,128)(2,1)S(1)}, u32[]{:S(2)}, u32[]{:S(2)}) collective-permute-start(bf16[256,1024]{1,0:T(8,128)(2,1)S(1)} %select_select_fusion.6.refs_3_), channel_id=1, source_target_pairs={{0,1},{1,0},{2,3},{3,2},{4,5},{5,4},{6,7},{7,6},{8,9},{9,8},{10,11... | collective-permute-start | bytes 1572872 | tf_op jit(solution)/shard_map/ppermute | solution.py:29
  114.7 26.5 %collective-permute-start.33 = (bf16[128,2048]{1,0:T(8,128)(2,1)S(1)}, bf16[128,2048]{1,0:T(8,128)(2,1)}, u32[]{:S(2)}, u32[]{:S(2)}) collective-permute-start(bf16[128,2048]{1,0:T(8,128)(2,1)S(1)} %collective-permute-done.18.refs_9_), channel_id=1, source_target_pairs={{0,16},{16,0},{1,17},{17,1},{2,18},{18,2},{3,19},{19,3},{4,20},{20... | collective-permute-start | bytes 1572872 | tf_op jit(solution)/shard_map/ppermute | solution.py:29
  116.2 23.0 %collective-permute-start.29 = (bf16[128,2048]{1,0:T(8,128)(2,1)S(1)}, bf16[128,2048]{1,0:T(8,128)(2,1)}, u32[]{:S(2)}, u32[]{:S(2)}) collective-permute-start(bf16[128,2048]{1,0:T(8,128)(2,1)S(1)} %copy-done.47), channel_id=1, source_target_pairs={{0,2},{1,3},{2,4},{3,5},{4,6},{5,7},{6,0},{7,1},{8,10},{9,11},{10,... | collective-permute-start | bytes 1572872 | tf_op jit(solution)/shard_map/ppermute | solution.py:29
  131.1 15.0 %collective-permute-start.37 = (bf16[128,2048]{1,0:T(8,128)(2,1)S(1)}, bf16[128,2048]{1,0:T(8,128)(2,1)}, u32[]{:S(2)}, u32[]{:S(2)}) collective-permute-start(bf16[128,2048]{1,0:T(8,128)(2,1)S(1)} %collective-permute-done.36.refs_13_), channel_id=1, source_target_pairs={{0,16},{16,0},{1,17},{17,1},{2,18},{18,2},{3,19},{19,3},{4,20},{20... | collective-permute-start | bytes 1572872 | tf_op jit(solution)/shard_map/ppermute | solution.py:29
  139.2 23.3 %collective-permute-start.30 = (bf16[128,2048]{1,0:T(8,128)(2,1)}, bf16[128,2048]{1,0:T(8,128)(2,1)}, u32[]{:S(2)}, u32[]{:S(2)}) collective-permute-start(bf16[128,2048]{1,0:T(8,128)(2,1)} %collective-permute-done.29.refs_5_), channel_id=1, source_target_pairs={{0,16},{16,0},{1,17},{17,1},{2,18},{18,2},{3,19},{19,3},{4,20},{20... | collective-permute-start | bytes 1572872 | tf_op jit(solution)/shard_map/ppermute | solution.py:29
  141.2 25.6 %collective-permute-start.34 = (bf16[128,2048]{1,0:T(8,128)(2,1)S(1)}, bf16[128,2048]{1,0:T(8,128)(2,1)}, u32[]{:S(2)}, u32[]{:S(2)}) collective-permute-start(bf16[128,2048]{1,0:T(8,128)(2,1)S(1)} %collective-permute-done.18.refs_9_), channel_id=1, source_target_pairs={{0,8},{8,0},{1,9},{9,1},{2,10},{10,2},{3,11},{11,3},{4,12},{12,4},... | collective-permute-start | bytes 1572872 | tf_op jit(solution)/shard_map/ppermute | solution.py:29
  141.2 21.4 %collective-permute-start.28 = (bf16[256,512]{1,0:T(8,128)(2,1)S(1)}, bf16[256,512]{1,0:T(8,128)(2,1)}, u32[]{:S(2)}, u32[]{:S(2)}) collective-permute-start(bf16[256,512]{1,0:T(8,128)(2,1)S(1)} %attend.2.refs_0_), channel_id=1, source_target_pairs={{0,6},{1,7},{2,0},{3,1},{4,2},{5,3},{6,4},{7,5},{8,14},{9,15},{10,... | collective-permute-start | bytes 786440 | tf_op jit(solution)/shard_map/ppermute | solution.py:29
  145.0 21.3 %collective-permute-start.27 = (bf16[256,512]{1,0:T(8,128)(2,1)S(1)}, bf16[256,512]{1,0:T(8,128)(2,1)}, u32[]{:S(2)}, u32[]{:S(2)}) collective-permute-start(bf16[256,512]{1,0:T(8,128)(2,1)S(1)} %attend.2.refs_0_), channel_id=1, source_target_pairs={{0,4},{1,5},{2,6},{3,7},{4,0},{5,1},{6,2},{7,3},{8,12},{9,13},{10,... | collective-permute-start | bytes 786440 | tf_op jit(solution)/shard_map/ppermute | solution.py:29
  146.1 20.2 %collective-permute-start.26 = (bf16[256,512]{1,0:T(8,128)(2,1)S(1)}, bf16[256,512]{1,0:T(8,128)(2,1)}, u32[]{:S(2)}, u32[]{:S(2)}) collective-permute-start(bf16[256,512]{1,0:T(8,128)(2,1)S(1)} %attend.2.refs_0_), channel_id=1, source_target_pairs={{0,2},{1,3},{2,4},{3,5},{4,6},{5,7},{6,0},{7,1},{8,10},{9,11},{10,... | collective-permute-start | bytes 786440 | tf_op jit(solution)/shard_map/ppermute | solution.py:29
  162.5 4.4 %collective-permute-start.35 = (bf16[128,2048]{1,0:T(8,128)(2,1)}, bf16[128,2048]{1,0:T(8,128)(2,1)S(1)}, u32[]{:S(2)}, u32[]{:S(2)}) collective-permute-start(bf16[128,2048]{1,0:T(8,128)(2,1)} %collective-permute-done.33.refs_10_), channel_id=1, source_target_pairs={{0,8},{8,0},{1,9},{9,1},{2,10},{10,2},{3,11},{11,3},{4,12},{12,4},... | collective-permute-start | bytes 1572872 | tf_op jit(solution)/shard_map/ppermute | solution.py:29
  162.5 4.4 %collective-permute-start.38 = (bf16[128,2048]{1,0:T(8,128)(2,1)S(1)}, bf16[128,2048]{1,0:T(8,128)(2,1)S(1)}, u32[]{:S(2)}, u32[]{:S(2)}) collective-permute-start(bf16[128,2048]{1,0:T(8,128)(2,1)S(1)} %collective-permute-done.36.refs_13_), channel_id=1, source_target_pairs={{0,8},{8,0},{1,9},{9,1},{2,10},{10,2},{3,11},{11,3},{4,12},{12,4},... | collective-permute-start | bytes 1572872 | tf_op jit(solution)/shard_map/ppermute | solution.py:29
  166.3 2.9 collective-permute-start.39
  166.3 2.9 collective-permute-start.31
  166.8 3.1 collective-permute-start.32
  177.1 14.3 %collective-permute-start.40 = (bf16[256,1024]{1,0:T(8,128)(2,1)}, bf16[256,1024]{1,0:T(8,128)(2,1)}, u32[]{:S(2)}, u32[]{:S(2)}) collective-permute-start(bf16[256,1024]{1,0:T(8,128)(2,1)} %code_terms.5), channel_id=1, source_target_pairs={{0,1},{1,0},{2,3},{3,2},{4,5},{5,4},{6,7},{7,6},{8,9},{9,8},{10,11... | collective-permute-start | bytes 1572872 | tf_op jit(solution)/shard_map/ppermute | solution.py:29
  177.6 20.7 %collective-permute-start.25 = (bf16[256,512]{1,0:T(8,128)(2,1)S(1)}, bf16[256,512]{1,0:T(8,128)(2,1)}, u32[]{:S(2)}, u32[]{:S(2)}) collective-permute-start(bf16[256,512]{1,0:T(8,128)(2,1)S(1)} %copy-done.10), channel_id=1, source_target_pairs={{0,6},{1,7},{2,0},{3,1},{4,2},{5,3},{6,4},{7,5},{8,14},{9,15},{10,... | collective-permute-start | bytes 786440 | tf_op jit(solution)/shard_map/ppermute | solution.py:29
  179.2 26.1 %collective-permute-start.24 = (bf16[256,512]{1,0:T(8,128)(2,1)S(1)}, bf16[256,512]{1,0:T(8,128)(2,1)}, u32[]{:S(2)}, u32[]{:S(2)}) collective-permute-start(bf16[256,512]{1,0:T(8,128)(2,1)S(1)} %copy-done.10), channel_id=1, source_target_pairs={{0,4},{1,5},{2,6},{3,7},{4,0},{5,1},{6,2},{7,3},{8,12},{9,13},{10,... | collective-permute-start | bytes 786440 | tf_op jit(solution)/shard_map/ppermute | solution.py:29
  181.3 23.9 %collective-permute-start.23 = (bf16[256,512]{1,0:T(8,128)(2,1)S(1)}, bf16[256,512]{1,0:T(8,128)(2,1)}, u32[]{:S(2)}, u32[]{:S(2)}) collective-permute-start(bf16[256,512]{1,0:T(8,128)(2,1)S(1)} %copy-done.10), channel_id=1, source_target_pairs={{0,2},{1,3},{2,4},{3,5},{4,6},{5,7},{6,0},{7,1},{8,10},{9,11},{10,... | collective-permute-start | bytes 786440 | tf_op jit(solution)/shard_map/ppermute | solution.py:29
  194.2 25.0 %collective-permute-start.44 = (bf16[256,1024]{1,0:T(8,128)(2,1)S(1)}, bf16[256,1024]{1,0:T(8,128)(2,1)S(1)}, u32[]{:S(2)}, u32[]{:S(2)}) collective-permute-start(bf16[256,1024]{1,0:T(8,128)(2,1)S(1)} %residual.2.refs_0_), channel_id=1, source_target_pairs={{0,1},{1,0},{2,3},{3,2},{4,5},{5,4},{6,7},{7,6},{8,9},{9,8},{10,11... | collective-permute-start | bytes 1572872 | tf_op jit(solution)/shard_map/ppermute | solution.py:29
  194.8 24.5 %collective-permute-start.43 = (bf16[256,1024]{1,0:T(8,128)(2,1)S(1)}, bf16[256,1024]{1,0:T(8,128)(2,1)S(1)}, u32[]{:S(2)}, u32[]{:S(2)}) collective-permute-start(bf16[256,1024]{1,0:T(8,128)(2,1)S(1)} %residual.2.refs_0_), channel_id=1, source_target_pairs={{0,2},{1,3},{2,4},{3,5},{4,6},{5,7},{8,10},{9,11},{10,12},{11,13},... | collective-permute-start | bytes 1572872 | tf_op jit(solution)/shard_map/ppermute | solution.py:29
  198.4 20.9 %collective-permute-start.42 = (bf16[256,1024]{1,0:T(8,128)(2,1)S(1)}, bf16[256,1024]{1,0:T(8,128)(2,1)S(1)}, u32[]{:S(2)}, u32[]{:S(2)}) collective-permute-start(bf16[256,1024]{1,0:T(8,128)(2,1)S(1)} %residual.2.refs_0_), channel_id=1, source_target_pairs={{2,0},{3,1},{4,2},{5,3},{6,4},{7,5},{10,8},{11,9},{12,10},{13,11},... | collective-permute-start | bytes 1572872 | tf_op jit(solution)/shard_map/ppermute | solution.py:29
  211.1 12.5 %collective-permute-start.41 = (bf16[256,1024]{1,0:T(8,128)(2,1)S(1)}, bf16[256,1024]{1,0:T(8,128)(2,1)S(1)}, u32[]{:S(2)}, u32[]{:S(2)}) collective-permute-start(bf16[256,1024]{1,0:T(8,128)(2,1)S(1)} %code_terms.6), channel_id=1, source_target_pairs={{0,1},{1,0},{2,3},{3,2},{4,5},{5,4},{6,7},{7,6},{8,9},{9,8},{10,11... | collective-permute-start | bytes 1572872 | tf_op jit(solution)/shard_map/ppermute | solution.py:29
  225.4 14.9 %collective-permute-start.47 = (bf16[256,1024]{1,0:T(8,128)(2,1)S(1)}, bf16[256,1024]{1,0:T(8,128)(2,1)S(1)}, u32[]{:S(2)}, u32[]{:S(2)}) collective-permute-start(bf16[256,1024]{1,0:T(8,128)(2,1)S(1)} %residual.3.refs_0_), channel_id=1, source_target_pairs={{0,1},{1,0},{2,3},{3,2},{4,5},{5,4},{6,7},{7,6},{8,9},{9,8},{10,11... | collective-permute-start | bytes 1572872 | tf_op jit(solution)/shard_map/ppermute | solution.py:29
  226.9 14.7 %collective-permute-start.46 = (bf16[256,1024]{1,0:T(8,128)(2,1)S(1)}, bf16[256,1024]{1,0:T(8,128)(2,1)S(1)}, u32[]{:S(2)}, u32[]{:S(2)}) collective-permute-start(bf16[256,1024]{1,0:T(8,128)(2,1)S(1)} %residual.3.refs_0_), channel_id=1, source_target_pairs={{0,2},{1,3},{2,4},{3,5},{4,6},{5,7},{8,10},{9,11},{10,12},{11,13},... | collective-permute-start | bytes 1572872 | tf_op jit(solution)/shard_map/ppermute | solution.py:29
  228.2 17.2 %collective-permute-start.45 = (bf16[256,1024]{1,0:T(8,128)(2,1)S(1)}, bf16[256,1024]{1,0:T(8,128)(2,1)S(1)}, u32[]{:S(2)}, u32[]{:S(2)}) collective-permute-start(bf16[256,1024]{1,0:T(8,128)(2,1)S(1)} %residual.3.refs_0_), channel_id=1, source_target_pairs={{2,0},{3,1},{4,2},{5,3},{6,4},{7,5},{10,8},{11,9},{12,10},{13,11},... | collective-permute-start | bytes 1572872 | tf_op jit(solution)/shard_map/ppermute | solution.py:29
  229.6 17.2 %collective-permute-start.56 = (bf16[256,1024]{1,0:T(8,128)(2,1)S(1)}, bf16[256,1024]{1,0:T(8,128)(2,1)S(1)}, u32[]{:S(2)}, u32[]{:S(2)}) collective-permute-start(bf16[256,1024]{1,0:T(8,128)(2,1)S(1)} %collective-permute-done.43), channel_id=1, source_target_pairs={{2,4},{3,5},{4,6},{5,7},{10,12},{11,13},{12,14},{13,15},{18,20},{1... | collective-permute-start | bytes 1572872 | tf_op jit(solution)/shard_map/ppermute | solution.py:29
  230.3 21.2 %collective-permute-start.57 = (bf16[256,1024]{1,0:T(8,128)(2,1)S(1)}, bf16[256,1024]{1,0:T(8,128)(2,1)S(1)}, u32[]{:S(2)}, u32[]{:S(2)}) collective-permute-start(bf16[256,1024]{1,0:T(8,128)(2,1)S(1)} %broadcast_select_fusion.refs_1_), channel_id=1, source_target_pairs={{0,1},{1,0},{2,3},{3,2},{4,5},{5,4},{6,7},{7,6},{8,9},{9,8},{10,11... | collective-permute-start | bytes 1572872 | tf_op jit(solution)/shard_map/ppermute | solution.py:29
  240.3 15.9 %collective-permute-start.55 = (bf16[256,1024]{1,0:T(8,128)(2,1)S(1)}, bf16[256,1024]{1,0:T(8,128)(2,1)S(1)}, u32[]{:S(2)}, u32[]{:S(2)}) collective-permute-start(bf16[256,1024]{1,0:T(8,128)(2,1)S(1)} %collective-permute-done.42), channel_id=1, source_target_pairs={{2,0},{3,1},{4,2},{5,3},{10,8},{11,9},{12,10},{13,11},{18,16},{19,... | collective-permute-start | bytes 1572872 | tf_op jit(solution)/shard_map/ppermute | solution.py:29
  245.5 12.6 %collective-permute-start.49 = (bf16[256,1024]{1,0:T(8,128)(2,1)S(1)}, bf16[256,1024]{1,0:T(8,128)(2,1)S(1)}, u32[]{:S(2)}, u32[]{:S(2)}) collective-permute-start(bf16[256,1024]{1,0:T(8,128)(2,1)S(1)} %collective-permute-done.46), channel_id=1, source_target_pairs={{2,4},{3,5},{4,6},{5,7},{10,12},{11,13},{12,14},{13,15},{18,20},{1... | collective-permute-start | bytes 1572872 | tf_op jit(solution)/shard_map/ppermute | solution.py:29
  246.2 16.5 %collective-permute-start.50 = (bf16[256,1024]{1,0:T(8,128)(2,1)S(1)}, bf16[256,1024]{1,0:T(8,128)(2,1)S(1)}, u32[]{:S(2)}, u32[]{:S(2)}) collective-permute-start(bf16[256,1024]{1,0:T(8,128)(2,1)S(1)} %broadcast_select_fusion.1.refs_1_), channel_id=1, source_target_pairs={{0,1},{1,0},{2,3},{3,2},{4,5},{5,4},{6,7},{7,6},{8,9},{9,8},{10,11... | collective-permute-start | bytes 1572872 | tf_op jit(solution)/shard_map/ppermute | solution.py:29
  246.8 22.2 %collective-permute-start.48 = (bf16[256,1024]{1,0:T(8,128)(2,1)S(1)}, bf16[256,1024]{1,0:T(8,128)(2,1)S(1)}, u32[]{:S(2)}, u32[]{:S(2)}) collective-permute-start(bf16[256,1024]{1,0:T(8,128)(2,1)S(1)} %collective-permute-done.45), channel_id=1, source_target_pairs={{2,0},{3,1},{4,2},{5,3},{10,8},{11,9},{12,10},{13,11},{18,16},{19,... | collective-permute-start | bytes 1572872 | tf_op jit(solution)/shard_map/ppermute | solution.py:29
  256.3 17.7 %collective-permute-start.60 = (bf16[256,1024]{1,0:T(8,128)(2,1)S(1)}, bf16[256,1024]{1,0:T(8,128)(2,1)S(1)}, u32[]{:S(2)}, u32[]{:S(2)}) collective-permute-start(bf16[256,1024]{1,0:T(8,128)(2,1)S(1)} %select_select_fusion.1.refs_2_), channel_id=1, source_target_pairs={{0,1},{1,0},{2,3},{3,2},{4,5},{5,4},{6,7},{7,6},{8,9},{9,8},{10,11... | collective-permute-start | bytes 1572872 | tf_op jit(solution)/shard_map/ppermute | solution.py:29
  256.9 23.4 %collective-permute-start.58 = (bf16[256,1024]{1,0:T(8,128)(2,1)S(1)}, bf16[256,1024]{1,0:T(8,128)(2,1)S(1)}, u32[]{:S(2)}, u32[]{:S(2)}) collective-permute-start(bf16[256,1024]{1,0:T(8,128)(2,1)S(1)} %collective-permute-done.55), channel_id=1, source_target_pairs={{2,0},{3,1},{10,8},{11,9},{18,16},{19,17},{26,24},{27,25}} | collective-permute-start | bytes 1572872 | tf_op jit(solution)/shard_map/ppermute | solution.py:29
  258.2 22.1 %collective-permute-start.59 = (bf16[256,1024]{1,0:T(8,128)(2,1)S(1)}, bf16[256,1024]{1,0:T(8,128)(2,1)S(1)}, u32[]{:S(2)}, u32[]{:S(2)}) collective-permute-start(bf16[256,1024]{1,0:T(8,128)(2,1)S(1)} %collective-permute-done.56), channel_id=1, source_target_pairs={{4,6},{5,7},{12,14},{13,15},{20,22},{21,23},{28,30},{29,31}} | collective-permute-start | bytes 1572872 | tf_op jit(solution)/shard_map/ppermute | solution.py:29
  269.1 12.7 %collective-permute-start.53 = (bf16[256,1024]{1,0:T(8,128)(2,1)S(1)}, bf16[256,1024]{1,0:T(8,128)(2,1)S(1)}, u32[]{:S(2)}, u32[]{:S(2)}) collective-permute-start(bf16[256,1024]{1,0:T(8,128)(2,1)S(1)} %select_select_fusion.3.refs_2_), channel_id=1, source_target_pairs={{0,1},{1,0},{2,3},{3,2},{4,5},{5,4},{6,7},{7,6},{8,9},{9,8},{10,11... | collective-permute-start | bytes 1572872 | tf_op jit(solution)/shard_map/ppermute | solution.py:29
  269.7 18.4 %collective-permute-start.51 = (bf16[256,1024]{1,0:T(8,128)(2,1)S(1)}, bf16[256,1024]{1,0:T(8,128)(2,1)S(1)}, u32[]{:S(2)}, u32[]{:S(2)}) collective-permute-start(bf16[256,1024]{1,0:T(8,128)(2,1)S(1)} %collective-permute-done.48), channel_id=1, source_target_pairs={{2,0},{3,1},{10,8},{11,9},{18,16},{19,17},{26,24},{27,25}} | collective-permute-start | bytes 1572872 | tf_op jit(solution)/shard_map/ppermute | solution.py:29
  274.0 14.1 %collective-permute-start.52 = (bf16[256,1024]{1,0:T(8,128)(2,1)S(1)}, bf16[256,1024]{1,0:T(8,128)(2,1)S(1)}, u32[]{:S(2)}, u32[]{:S(2)}) collective-permute-start(bf16[256,1024]{1,0:T(8,128)(2,1)S(1)} %collective-permute-done.49), channel_id=1, source_target_pairs={{4,6},{5,7},{12,14},{13,15},{20,22},{21,23},{28,30},{29,31}} | collective-permute-start | bytes 1572872 | tf_op jit(solution)/shard_map/ppermute | solution.py:29
  288.5 14.9 %collective-permute-start.61 = (bf16[256,1024]{1,0:T(8,128)(2,1)S(1)}, bf16[256,1024]{1,0:T(8,128)(2,1)S(1)}, u32[]{:S(2)}, u32[]{:S(2)}) collective-permute-start(bf16[256,1024]{1,0:T(8,128)(2,1)S(1)} %get-tuple-element.200.refs_3_), channel_id=1, source_target_pairs={{0,1},{1,0},{2,3},{3,2},{4,5},{5,4},{6,7},{7,6},{8,9},{9,8},{10,11... | collective-permute-start | bytes 1572872 | tf_op jit(solution)/shard_map/ppermute | solution.py:29
  289.0 22.7 %collective-permute-start.54 = (bf16[256,1024]{1,0:T(8,128)(2,1)S(1)}, bf16[256,1024]{1,0:T(8,128)(2,1)S(1)}, u32[]{:S(2)}, u32[]{:S(2)}) collective-permute-start(bf16[256,1024]{1,0:T(8,128)(2,1)S(1)} %get-tuple-element.185.refs_3_), channel_id=1, source_target_pairs={{0,1},{1,0},{2,3},{3,2},{4,5},{5,4},{6,7},{7,6},{8,9},{9,8},{10,11... | collective-permute-start | bytes 1572872 | tf_op jit(solution)/shard_map/ppermute | solution.py:29
  (48 other events, 1039.2 us)
